TPU v7x, 32 devices: a whole 2x2x4 slice. The times are simulated.
32 devices in a mesh: seq: 8 (over z, x), dp: 4 (over y, core).
Axes of the slice: x: 2, y: 2, z: 4, core: 2. Of those that a mesh axis runs over, the one named last changes fastest.
Arguments:
- inputs: bfloat16 [16, 1024, 768], P('dp', 'seq'), may hold values from -6 to 6
- lengths: int32 [16], P('dp'), may hold values from 1 to 1024, as said below
- norm_gain: float32 [768], replicated, may hold values from 0.25 to 1.75
- norm_bias: float32 [768], replicated, may hold values from -3 to 3
- mixer_in: bfloat16 [768, 2304], replicated, may hold values from -0.21875 to 0.21875
- filter_in: float32 [33, 64], replicated, may hold values from -64 to 64
- filter_in_bias: float32 [64], replicated, may hold values from -3.140625 to 3.140625
- filter_mid: float32 [64, 64], replicated, may hold values from -0.75 to 0.75
- filter_mid_bias: float32 [64], replicated, may hold values from -3.140625 to 3.140625
- filter_out: float32 [64, 768], replicated, may hold values from -0.03125 to 0.03125
- mixer_out: bfloat16 [768, 768], replicated, may hold values from -0.21875 to 0.21875
- second_gain: float32 [768], replicated, may hold values from 0.25 to 1.75
- second_bias: float32 [768], replicated, may hold values from -3 to 3
- up_weight: bfloat16 [768, 3072], replicated, may hold values from -0.21875 to 0.21875
- down_weight: bfloat16 [3072, 768], replicated, may hold values from -0.109375 to 0.109375
- cotangent: bfloat16 [16, 1024, 768], P('dp', 'seq'), may hold values from -6 to 6
Outputs:
- output: bfloat16 [16, 1024, 768], P('dp', 'seq')
- grad_inputs: float32 [16, 1024, 768], P('dp', 'seq')
- grad_norm_gain: float32 [768], replicated
- grad_norm_bias: float32 [768], replicated
- grad_mixer_in: float32 [768, 2304], replicated
- grad_filter_in: float32 [33, 64], replicated
- grad_filter_in_bias: float32 [64], replicated
- grad_filter_mid: float32 [64, 64], replicated
- grad_filter_mid_bias: float32 [64], replicated
- grad_filter_out: float32 [64, 768], replicated
- grad_mixer_out: float32 [768, 768], replicated
- grad_second_gain: float32 [768], replicated
- grad_second_bias: float32 [768], replicated
- grad_up_weight: float32 [768, 3072], replicated
- grad_down_weight: float32 [3072, 768], replicated
Inputs may be any that keep to these rules, and one draw needn't show every extreme that they name: `lengths`: in every aligned block of 4 sequences (those of one index of dp) at least one sequence has length 1024.
All inputs are finite; a program needn't handle non-finite values.
Results may differ from a plain program's by a relative error of at most 0.012.
Values may be sent and summed in bfloat16 or wider, within the bound.
No kernel may reach another device: no remote copies, remote signals or barrier semaphores. Data moves between devices by JAX's collectives and lax.ppermute only.
A program may use at most 256 MiB of HBM per device.

v0:
```python
import math

import jax
import jax.numpy as jnp
from jax import lax
from jax.sharding import PartitionSpec as P

KL = 2048
BANDS = 16
LAGS = 16


HIGH = lax.Precision.HIGHEST
EPSILON = 1e-05


def shifted(value, axis, by):
    devices = lax.axis_size(axis)
    pairs = [(i, i + by) for i in range(devices) if 0 <= i + by < devices]
    return lax.ppermute(value, axis, pairs)


def layer_norm(values, gain, shift):
    center = values - jnp.mean(values, axis=-1, keepdims=True)
    spread = jnp.mean(center * center, axis=-1, keepdims=True)
    return center * lax.rsqrt(spread + EPSILON) * gain + shift


def feature_table(taps, bands):
    steps = jnp.arange(taps, dtype=jnp.float32) / taps
    freqs = jnp.arange(1, bands + 1, dtype=jnp.float32)
    phase = 2.0 * math.pi * steps[:, None] * freqs[None, :]
    return jnp.concatenate([steps[:, None], jnp.cos(phase), jnp.sin(phase)], axis=1)


def filter_kernel(filter_in, filter_in_bias, filter_mid, filter_mid_bias, filter_out):
    table = feature_table(KL, BANDS)
    first = jnp.sin(jnp.dot(table, filter_in, precision=HIGH) + filter_in_bias)
    second = jnp.sin(jnp.dot(first, filter_mid, precision=HIGH) + filter_mid_bias)
    return jnp.dot(second, filter_out, precision=HIGH)


def dft_tables(block_len):
    length = 2 * block_len
    index = jnp.arange(length, dtype=jnp.int32)
    angle = (index[:, None] * index[None, :] % length).astype(jnp.float32) * (
        2.0 * math.pi / length
    )
    return (jnp.cos(angle), jnp.sin(angle))


def split_table(table):
    leading = table.astype(jnp.bfloat16)
    remainder = (table - leading.astype(jnp.float32)).astype(jnp.bfloat16)
    return (leading, remainder)


def low_tables(cos_t, sin_t):
    length = cos_t.shape[0]
    half = length // 2
    return (
        split_table(cos_t[:, :half]),
        split_table(sin_t[:, :half]),
        split_table(cos_t[half:] / length),
        split_table(sin_t[half:] / length),
    )


def apply_split(pattern, halves, values):
    first = jnp.einsum(pattern, halves[0], values, preferred_element_type=jnp.float32)
    second = jnp.einsum(pattern, halves[1], values, preferred_element_type=jnp.float32)
    return first + second


def kernel_freq(kernel, cos_t, sin_t):
    block_len = cos_t.shape[0] // 2
    width = kernel.shape[1]
    count = kernel.shape[0] // block_len
    padded = jnp.concatenate(
        [
            jnp.zeros((block_len, width), jnp.float32),
            kernel,
            jnp.zeros((2 * block_len, width), jnp.float32),
        ],
        axis=0,
    )
    pieces = padded.reshape(count + 3, block_len, width)
    segments = jnp.concatenate([pieces[: count + 1], pieces[1 : count + 2]], axis=1)
    real = jnp.einsum("fn,mnd->mfd", cos_t, segments, precision=HIGH)
    imag = -jnp.einsum("fn,mnd->mfd", sin_t, segments, precision=HIGH)
    return (real, imag)


def to_freq(values, tables):
    real = apply_split("fc,scd->sfd", tables[0], values)
    imag = -apply_split("fc,scd->sfd", tables[1], values)
    return (real, imag)


def from_freq(real, imag, cos_t, sin_t):
    length = cos_t.shape[0]
    half = length // 2
    first = jnp.einsum("nf,sfd->snd", cos_t[half:], real, precision=HIGH)
    second = jnp.einsum("nf,sfd->snd", sin_t[half:], imag, precision=HIGH)
    return (first - second) / length


def grad_freq(values, tables):
    real = apply_split("nf,snd->sfd", tables[2], values)
    imag = -apply_split("nf,snd->sfd", tables[3], values)
    return (real, imag)


def grad_time(real, imag, cos_t, sin_t):
    half = cos_t.shape[0] // 2
    first = jnp.einsum("fc,sfd->scd", cos_t[:, :half], real, precision=HIGH)
    second = jnp.einsum("fc,sfd->scd", sin_t[:, :half], imag, precision=HIGH)
    return first - second


def add_forward(acc, k_real, k_imag, values, tables):
    z_real, z_imag = to_freq(values, tables)
    return (acc[0] + k_real * z_real - k_imag * z_imag, acc[1] + k_real * z_imag + k_imag * z_real)


def add_backward(acc, k_real, k_imag, grads, own_real, own_imag, tables):
    d_real, d_imag = grad_freq(grads, tables)
    new_real = acc[0] + k_real * d_real + k_imag * d_imag
    new_imag = acc[1] - k_imag * d_real + k_real * d_imag
    term_real = jnp.sum(own_real * d_real + own_imag * d_imag, axis=0)
    term_imag = jnp.sum(own_real * d_imag - own_imag * d_real, axis=0)
    return ((new_real, new_imag), (term_real, term_imag))


def forward_stack(stack, k_real, k_imag, acc, tables):

    def forward_step(carry, item):
        return (add_forward(carry, item[1], item[2], item[0], tables), None)

    result, _ = lax.scan(forward_step, acc, (stack, k_real, k_imag))
    return result


def backward_stack(stack, k_real, k_imag, acc, own_real, own_imag, tables):

    def backward_step(carry, item):
        return add_backward(carry, item[1], item[2], item[0], own_real, own_imag, tables)

    return lax.scan(backward_step, acc, (stack, k_real, k_imag))


def sum_everywhere(parts):
    flat_grads = jnp.concatenate([piece.reshape(-1) for piece in parts])
    portion = lax.psum_scatter(flat_grads, ("seq", "dp"), scatter_dimension=0, tiled=True)
    summed = lax.all_gather(portion.astype(jnp.bfloat16), ("seq", "dp"), axis=0, tiled=True).astype(
        portion.dtype
    )
    results = []
    offset = 0
    for piece in parts:
        results.append(summed[offset : offset + piece.size].reshape(piece.shape))
        offset = offset + piece.size
    return results


def local(
    inputs,
    lengths,
    norm_gain,
    norm_bias,
    mixer_in,
    filter_in,
    filter_in_bias,
    filter_mid,
    filter_mid_bias,
    filter_out,
    mixer_out,
    second_gain,
    second_bias,
    up_weight,
    down_weight,
    cotangent,
):
    seqs, block_len, width = inputs.shape
    row_count = seqs * block_len
    reach = min(LAGS, lax.axis_size("seq") - 1)
    rank = lax.axis_index("seq")
    position = rank * block_len + jnp.arange(block_len, dtype=jnp.int32)
    valid = (position[None, :] < lengths[:, None]).astype(jnp.float32)[:, :, None]
    cos_t, sin_t = dft_tables(block_len)
    tables = low_tables(cos_t, sin_t)
    kernel, filter_back = jax.vjp(
        filter_kernel, filter_in, filter_in_bias, filter_mid, filter_mid_bias, filter_out
    )
    k_real, k_imag = kernel_freq(kernel, cos_t, sin_t)
    x_full = inputs.astype(jnp.float32).reshape(row_count, width)
    normed = layer_norm(x_full, norm_gain, norm_bias).astype(jnp.bfloat16)
    projected = jnp.dot(normed, mixer_in, preferred_element_type=jnp.float32)
    value = projected[:, :width]
    gate_a = projected[:, width : 2 * width]
    gate_b = projected[:, 2 * width :]
    gated = (value * gate_a).astype(jnp.bfloat16).reshape(seqs, block_len, width) * valid.astype(
        jnp.bfloat16
    )
    own_real, own_imag = to_freq(gated, tables)
    initial = (
        k_real[0] * own_real - k_imag[0] * own_imag,
        k_real[0] * own_imag + k_imag[0] * own_real,
    )
    earlier = []
    for lag in range(1, reach + 1):
        earlier.append(shifted(gated, "seq", lag))
    y_real, y_imag = forward_stack(
        jnp.stack(earlier), k_real[1 : reach + 1], k_imag[1 : reach + 1], initial, tables
    )
    mixed = from_freq(y_real, y_imag, cos_t, sin_t).reshape(row_count, width)
    gated_out = (gate_b * mixed).astype(jnp.bfloat16)
    middle = x_full + jnp.dot(gated_out, mixer_out, preferred_element_type=jnp.float32)
    second_normed = layer_norm(middle, second_gain, second_bias).astype(jnp.bfloat16)
    pre = jnp.dot(second_normed, up_weight, preferred_element_type=jnp.float32)
    activated = jax.nn.gelu(pre, approximate=True).astype(jnp.bfloat16)
    result = middle + jnp.dot(activated, down_weight, preferred_element_type=jnp.float32)
    output = result.astype(jnp.bfloat16).reshape(seqs, block_len, width)
    upstream_low = cotangent.reshape(row_count, width)
    upstream = upstream_low.astype(jnp.float32)
    grad_down = jnp.einsum("rk,rd->kd", activated, upstream_low, preferred_element_type=jnp.float32)
    d_act = jnp.einsum("rd,kd->rk", upstream_low, down_weight, preferred_element_type=jnp.float32)
    _, gelu_back = jax.vjp(lambda arg: jax.nn.gelu(arg, approximate=True), pre)
    d_pre = gelu_back(d_act)[0].astype(jnp.bfloat16)
    grad_up = jnp.einsum("rd,rk->dk", second_normed, d_pre, preferred_element_type=jnp.float32)
    d_second = jnp.einsum("rk,dk->rd", d_pre, up_weight, preferred_element_type=jnp.float32)
    _, second_back = jax.vjp(layer_norm, middle, second_gain, second_bias)
    d_middle_norm, grad_second_gain, grad_second_bias = second_back(d_second)
    d_middle = upstream + d_middle_norm
    d_middle_low = d_middle.astype(jnp.bfloat16)
    grad_mixer_out = jnp.einsum(
        "rk,rd->kd", gated_out, d_middle_low, preferred_element_type=jnp.float32
    )
    d_gated_out = jnp.einsum(
        "rd,kd->rk", d_middle_low, mixer_out, preferred_element_type=jnp.float32
    )
    d_gate_b = d_gated_out * mixed
    d_mixed = (d_gated_out * gate_b).astype(jnp.bfloat16).reshape(seqs, block_len, width)
    empty_freq = jnp.zeros((seqs, 2 * block_len, width), jnp.float32)
    start_acc, own_terms = add_backward(
        (empty_freq, empty_freq), k_real[0], k_imag[0], d_mixed, own_real, own_imag, tables
    )
    unused = jnp.zeros((LAGS - reach, 2 * block_len, width), jnp.float32)
    later = []
    for lead in range(1, reach + 1):
        later.append(shifted(d_mixed, "seq", -lead))
    (z_real, z_imag), terms = backward_stack(
        jnp.stack(later),
        k_real[1 : reach + 1],
        k_imag[1 : reach + 1],
        start_acc,
        own_real,
        own_imag,
        tables,
    )
    dk_real = jnp.concatenate([own_terms[0][None], terms[0], unused], axis=0)
    dk_imag = jnp.concatenate([own_terms[1][None], terms[1], unused], axis=0)
    d_gated = (grad_time(z_real, z_imag, cos_t, sin_t) * valid).reshape(row_count, width)
    d_projected = jnp.concatenate([d_gated * gate_a, d_gated * value, d_gate_b], axis=1).astype(
        jnp.bfloat16
    )
    grad_mixer_in = jnp.einsum("rd,rk->dk", normed, d_projected, preferred_element_type=jnp.float32)
    d_normed = jnp.einsum("rk,dk->rd", d_projected, mixer_in, preferred_element_type=jnp.float32)
    _, first_back = jax.vjp(layer_norm, x_full, norm_gain, norm_bias)
    d_x_norm, grad_norm_gain, grad_norm_bias = first_back(d_normed)
    grad_inputs = (d_middle + d_x_norm).reshape(seqs, block_len, width)
    _, kernel_back = jax.vjp(lambda kern: kernel_freq(kern, cos_t, sin_t), kernel)
    d_kernel = kernel_back((dk_real, dk_imag))[0]
    dense = [
        grad_norm_gain,
        grad_norm_bias,
        grad_mixer_in,
        grad_mixer_out,
        grad_second_gain,
        grad_second_bias,
        grad_up,
        grad_down,
    ]
    summed = sum_everywhere([d_kernel] + dense)
    filter_grads = filter_back(summed[0])
    dense_sums = summed[1:]
    return (
        output,
        grad_inputs,
        dense_sums[0],
        dense_sums[1],
        dense_sums[2],
        filter_grads[0],
        filter_grads[1],
        filter_grads[2],
        filter_grads[3],
        filter_grads[4],
        dense_sums[3],
        dense_sums[4],
        dense_sums[5],
        dense_sums[6],
        dense_sums[7],
    )


def solution(mesh):
    in_specs = (
        P("dp", "seq", None),
        P("dp"),
        P(),
        P(),
        P(),
        P(),
        P(),
        P(),
        P(),
        P(),
        P(),
        P(),
        P(),
        P(),
        P(),
        P("dp", "seq", None),
    )
    out_specs = (
        P("dp", "seq", None),
        P("dp", "seq", None),
        P(),
        P(),
        P(),
        P(),
        P(),
        P(),
        P(),
        P(),
        P(),
        P(),
        P(),
        P(),
        P(),
    )
    return jax.shard_map(local, mesh=mesh, in_specs=in_specs, out_specs=out_specs, check_vma=False)
```

profile of v0, /device:TPU:31, one launch (start us, length us, event | category | flops | bytes accessed | tf_op | source)
XLA Modules:
  0.0 1756.0 jit_solution(3400545078319877575)
XLA Ops:
  33.7 4.2 fusion.173
  42.7 7.0 fusion.179
  49.7 10.5 fusion.172
  60.2 7.4 copy.76
  67.6 7.4 copy.77
  75.0 18.4 %fusion.60 = f32[17,256,768]{1,2,0:T(8,128)} fusion(f32[17,128,768]{1,2,0:T(8,128)} %copy.77, f32[17,128,768]{1,2,0:T(8,128)} %copy.76), kind=kOutput, calls=%fused_computation.88 | convolution fusion | flops 10271916032 | bytes 26738688 | tf_op jit(solution)/shard_map/fn,mnd->mfd/dot_general | solution.py:89
  93.4 16.2 negate_bitcast_fusion
  117.7 6.8 multiply_add_fusion
  124.5 4.5 fusion.180
  130.9 5.5 slice.189
  136.4 5.5 slice.190
  153.0 18.3 %collective-permute-done.5 = bf16[4,128,768]{1,2,0:T(8,128)(2,1)S(1)} collective-permute-done((bf16[4,128,768]{1,2,0:T(8,128)(2,1)}, bf16[4,128,768]{1,2,0:T(8,128)(2,1)S(1)}, u32[]{:S(2)}, u32[]{:S(2)}) %collective-permute-start.5) | collective-permute-done | bytes 786464 | tf_op jit(solution)/shard_map/ppermute | solution.py:20
  171.4 16.7 collective-permute-done.6
  190.6 100.4 %while.28 = (s32[]{:T(128)}, f32[4,256,768]{1,2,0:T(8,128)}, f32[4,256,768]{1,2,0:T(8,128)}, f32[7,256,768]{1,2,0:T(8,128)}, bf16[7,4,128,768]{2,3,1,0:T(8,128)(...) while((s32[]{:T(128)}, f32[4,256,768]{1,2,0:T(8,128)}, ...), condition=%wide.region_3.4_spmd, body=%wide.region_2.3_spmd.sunk | while | flops 813957120 | bytes 90704184 | solution.py:140
  198.2 3.8 fusion.254
  212.5 3.8 fusion.254
  226.7 3.8 fusion.254
  255.3 3.8 fusion.254
  283.9 3.8 fusion.254
  291.0 5.4 fusion.109
  304.8 9.0 fusion.69
  338.3 9.8 fusion.164
  351.2 5.6 fusion.70
  359.8 5.9 copy.109
  371.2 10.7 reshape.293
  389.5 4.6 collective-permute-done.11
  395.4 15.6 collective-permute-done.12
  411.1 16.7 collective-permute-done.13
  430.4 138.6 %while.29 = (s32[]{:T(128)}, f32[4,256,768]{1,2,0:T(8,128)}, f32[4,256,768]{1,2,0:T(8,128)}, f32[7,256,768]{1,2,0:T(8,128)}, f32[7,256,768]{1,2,0:T(8,128)}, /*i...) while((s32[]{:T(128)}, f32[4,256,768]{1,2,0:T(8,128)}, ...), condition=%wide.region_11.12_spmd, body=%wide.region_8.11_spmd.sunk | while | flops 819855360 | bytes 126880664 | solution.py:149
  438.7 5.5 fusion.263
  458.5 5.5 fusion.263
  478.2 5.5 fusion.263
  498.0 5.5 fusion.263
  517.7 5.5 fusion.263
  537.4 5.5 fusion.263
  557.2 5.5 fusion.263
  569.1 5.4 fusion.106
  579.4 5.0 fusion.92
  584.5 3.8 fusion.165
  588.3 7.9 reshape.290
  596.2 17.6 %fusion.49 = f32[17,768,256]{2,1,0:T(8,128)} fusion(f32[7,256,768]{1,2,0:T(8,128)} %get-tuple-element.147, f32[1,256,768]{1,2,0:T(8,128)} %bitcast.426, f32[17]{0:T(128)S(1)} %copy-done.99), kind=kOutput, calls=%fused_computation.73 | convolution fusion | flops 10278600704 | bytes 19660868 | tf_op jit(solution)/shard_map/transpose(jvp(fn,mnd->mfd))/dot_general | solution.py:90
  613.8 18.9 %add_bitcast_fusion = f32[17,256,768]{1,2,0:T(8,128)} fusion(f32[17,768,256]{2,1,0:T(8,128)} %fusion.49, f32[7,256,768]{1,2,0:T(8,128)S(1)} %bitcast.420, f32[1,256,768]{1,2,0:T(8,128)S(1)} %bitcast.421, f32[17]{0:T(128)S(1)} %copy-done.99), kind=kOutput, calls=%fused_computation.82 | convolution fusion | flops 10278600704 | bytes 33030212 | tf_op jit(solution)/shard_map/transpose(jvp(fn,mnd->mfd))/dot_general | solution.py:89
  632.8 11.2 fusion.171
  644.0 8.0 pad_add_fusion
  652.0 6.6 copy.96
  658.6 6.8 reshape.289
  665.5 4.8 constant_dynamic-update-slice_fusion
  674.3 60.8 %dynamic-update-slice.4 = f32[8653824]{0:T(1024)} dynamic-update-slice(f32[8653824]{0:T(1024)} %constant_dynamic-update-slice_fusion.5, f32[1769472]{0:T(1024)} %reshape.290, s32[]{} %constant.113) | dynamic-update-slice | bytes 14155780
  735.1 21.3 %dynamic-update-slice.5 = f32[8653824]{0:T(1024)} dynamic-update-slice(f32[8653824]{0:T(1024)} %dynamic-update-slice.4, f32[589824]{0:T(1024)} %reshape.291, s32[]{} %constant.114) | dynamic-update-slice | bytes 4718596
  759.0 8.3 constant_dynamic-update-slice_fusion.2
  767.3 8.3 constant_dynamic-update-slice_fusion.1
  775.6 591.6 %all-reduce.10 = bf16[8653824]{0:T(1024)(128)(2,1)} all-reduce(f32[8653824]{0:T(1024)} %constant_dynamic-update-slice_fusion.1), channel_id=2, replica_groups=mesh['seq'=8,'dp'=4] {'seq','dp'}, use_global_device_ids=true, to_apply=%region_20.21.clone | all-reduce | flops 8653824 | bytes 51922944
  1369.4 6.1 broadcast.205
  1375.5 9.4 dynamic-update-slice
  1385.0 9.4 add_convert_fusion
  1396.3 275.7 %all-reduce.9.cloned.1.call-done = bf16[8653824]{0:T(1024)(128)(2,1)} async-done(((bf16[8653824]{0:T(1024)(128)(2,1)}), bf16[8653824]{0:T(1024)(128)(2,1)}) %all-reduce.9.cloned.1.call-update) | async-done | bytes 17307664
  1671.9 9.6 fusion.169
  1681.6 10.9 slice.179
  1692.5 11.3 slice.181
  1703.7 4.7 slice.195
  1708.5 8.2 reshape.294
  1719.8 6.4 slice.173
  1726.2 4.6 fusion.183
  1730.9 4.8 fusion.177
  (594 shorter events, 321.1 us)
Async XLA Ops:
  7.2 1664.8 %all-reduce.9.cloned.1.call-start = ((), (), s32[]{:S(2)}) async-start(), calls=%async_computation | async-start | bytes 34615296
  17.2 16.5 copy-start.97
  18.2 20.5 %copy-start.98 = (f32[64]{0:T(128)S(1)}, f32[64]{0:T(128)}, u32[]{:S(2)}) copy-start(f32[64]{0:T(128)} %param.28) | copy-start | bytes 772
  20.5 18.2 %copy-start.79 = (f32[64,64]{1,0:T(8,128)S(1)}, f32[64,64]{1,0:T(8,128)}, u32[]{:S(2)}) copy-start(f32[64,64]{1,0:T(8,128)} %param.27) | copy-start | bytes 49156
  20.5 22.2 %copy-start.75 = (f32[64,768]{1,0:T(8,128)S(1)}, f32[64,768]{1,0:T(8,128)}, u32[]{:S(2)}) copy-start(f32[64,768]{1,0:T(8,128)} %param.29) | copy-start | bytes 589828
  23.2 121.0 %collective-permute-start = (bf16[4,128,768]{1,2,0:T(8,128)(2,1)}, bf16[4,128,768]{1,2,0:T(8,128)(2,1)}, u32[]{:S(2)}, u32[]{:S(2)}) collective-permute-start(bf16[4,128,768]{1,2,0:T(8,128)(2,1)} %broadcast_multiply_fusion), channel_id=1, source_target_pairs={{0,4},{4,8},{8,12},{12,16},{16,20},{20,24},{24,28},{1,5},{5,9},{9,... | collective-permute-start | bytes 2359304 | tf_op jit(solution)/shard_map/ppermute | solution.py:20
  24.5 122.2 %collective-permute-start.1 = (bf16[4,128,768]{1,2,0:T(8,128)(2,1)}, bf16[4,128,768]{1,2,0:T(8,128)(2,1)}, u32[]{:S(2)}, u32[]{:S(2)}) collective-permute-start(bf16[4,128,768]{1,2,0:T(8,128)(2,1)} %broadcast_multiply_fusion), channel_id=1, source_target_pairs={{0,8},{4,12},{8,16},{12,20},{16,24},{20,28},{1,9},{5,13},{9,17},{1... | collective-permute-start | bytes 2359304 | tf_op jit(solution)/shard_map/ppermute | solution.py:20
  25.8 123.4 %collective-permute-start.2 = (bf16[4,128,768]{1,2,0:T(8,128)(2,1)}, bf16[4,128,768]{1,2,0:T(8,128)(2,1)}, u32[]{:S(2)}, u32[]{:S(2)}) collective-permute-start(bf16[4,128,768]{1,2,0:T(8,128)(2,1)} %broadcast_multiply_fusion), channel_id=1, source_target_pairs={{0,12},{4,16},{8,20},{12,24},{16,28},{1,13},{5,17},{9,21},{13,25},... | collective-permute-start | bytes 2359304 | tf_op jit(solution)/shard_map/ppermute | solution.py:20
  27.1 123.4 %collective-permute-start.3 = (bf16[4,128,768]{1,2,0:T(8,128)(2,1)}, bf16[4,128,768]{1,2,0:T(8,128)(2,1)}, u32[]{:S(2)}, u32[]{:S(2)}) collective-permute-start(bf16[4,128,768]{1,2,0:T(8,128)(2,1)} %broadcast_multiply_fusion), channel_id=1, source_target_pairs={{0,16},{4,20},{8,24},{12,28},{1,17},{5,21},{9,25},{13,29},{2,18},{... | collective-permute-start | bytes 2359304 | tf_op jit(solution)/shard_map/ppermute | solution.py:20
  28.4 123.3 %collective-permute-start.4 = (bf16[4,128,768]{1,2,0:T(8,128)(2,1)}, bf16[4,128,768]{1,2,0:T(8,128)(2,1)}, u32[]{:S(2)}, u32[]{:S(2)}) collective-permute-start(bf16[4,128,768]{1,2,0:T(8,128)(2,1)} %broadcast_multiply_fusion), channel_id=1, source_target_pairs={{0,20},{4,24},{8,28},{1,21},{5,25},{9,29},{2,22},{6,26},{10,30},{3... | collective-permute-start | bytes 2359304 | tf_op jit(solution)/shard_map/ppermute | solution.py:20
  33.1 8.8 copy-start.81
  33.6 8.2 copy-start.70
  33.7 8.2 copy-start.72
  75.0 18.5 %copy-start.14 = (f32[17,128,768]{1,2,0:T(8,128)S(1)}, f32[17,128,768]{1,2,0:T(8,128)}, u32[]{:S(2)}) copy-start(f32[17,128,768]{1,2,0:T(8,128)} %copy.76) | copy-start | bytes 20054020
  75.0 18.5 %copy-start.15 = (f32[17,128,768]{1,2,0:T(8,128)S(1)}, f32[17,128,768]{1,2,0:T(8,128)}, u32[]{:S(2)}) copy-start(f32[17,128,768]{1,2,0:T(8,128)} %copy.77) | copy-start | bytes 20054020
  93.4 16.2 copy-start.63
  93.4 16.2 copy-start.66
  109.7 7.9 copy-start.49
  115.0 14.1 copy-start.16
  115.0 9.5 slice-start.4
  117.6 6.8 copy-start.31
  117.6 6.8 copy-start.33
  117.7 6.8 copy-start.59
  117.7 6.8 slice-start.5
  144.2 27.1 %collective-permute-start.5 = (bf16[4,128,768]{1,2,0:T(8,128)(2,1)}, bf16[4,128,768]{1,2,0:T(8,128)(2,1)S(1)}, u32[]{:S(2)}, u32[]{:S(2)}) collective-permute-start(bf16[4,128,768]{1,2,0:T(8,128)(2,1)} %broadcast_multiply_fusion), channel_id=1, source_target_pairs={{0,24},{4,28},{1,25},{5,29},{2,26},{6,30},{3,27},{7,31}} | collective-permute-start | bytes 2359304 | tf_op jit(solution)/shard_map/ppermute | solution.py:20
  146.7 41.4 %collective-permute-start.6 = (bf16[4,128,768]{1,2,0:T(8,128)(2,1)}, bf16[4,128,768]{1,2,0:T(8,128)(2,1)S(1)}, u32[]{:S(2)}, u32[]{:S(2)}) collective-permute-start(bf16[4,128,768]{1,2,0:T(8,128)(2,1)} %broadcast_multiply_fusion), channel_id=1, source_target_pairs={{0,28},{1,29},{2,30},{3,31}} | collective-permute-start | bytes 2359304 | tf_op jit(solution)/shard_map/ppermute | solution.py:20
  296.5 6.7 slice-start.2
  302.8 14.5 copy-start.37
  324.7 13.0 copy-start.20
  324.7 13.0 copy-start.57
  324.7 57.2 %collective-permute-start.7 = (bf16[4,128,768]{1,2,0:T(8,128)(2,1)}, bf16[4,128,768]{1,2,0:T(8,128)(2,1)}, u32[]{:S(2)}, u32[]{:S(2)}) collective-permute-start(bf16[4,128,768]{1,2,0:T(8,128)(2,1)} %copy.85), channel_id=1, source_target_pairs={{4,0},{8,4},{12,8},{16,12},{20,16},{24,20},{28,24},{5,1},{9,5},{13... | collective-permute-start | bytes 2359304 | tf_op jit(solution)/shard_map/ppermute | solution.py:20
  327.0 57.4 %collective-permute-start.8 = (bf16[4,128,768]{1,2,0:T(8,128)(2,1)}, bf16[4,128,768]{1,2,0:T(8,128)(2,1)}, u32[]{:S(2)}, u32[]{:S(2)}) collective-permute-start(bf16[4,128,768]{1,2,0:T(8,128)(2,1)} %copy.85), channel_id=1, source_target_pairs={{8,0},{12,4},{16,8},{20,12},{24,16},{28,20},{9,1},{13,5},{17,9},{2... | collective-permute-start | bytes 2359304 | tf_op jit(solution)/shard_map/ppermute | solution.py:20
  329.3 57.7 %collective-permute-start.9 = (bf16[4,128,768]{1,2,0:T(8,128)(2,1)}, bf16[4,128,768]{1,2,0:T(8,128)(2,1)}, u32[]{:S(2)}, u32[]{:S(2)}) collective-permute-start(bf16[4,128,768]{1,2,0:T(8,128)(2,1)} %copy.85), channel_id=1, source_target_pairs={{12,0},{16,4},{20,8},{24,12},{28,16},{13,1},{17,5},{21,9},{25,13},... | collective-permute-start | bytes 2359304 | tf_op jit(solution)/shard_map/ppermute | solution.py:20
  331.5 56.7 %collective-permute-start.10 = (bf16[4,128,768]{1,2,0:T(8,128)(2,1)}, bf16[4,128,768]{1,2,0:T(8,128)(2,1)}, u32[]{:S(2)}, u32[]{:S(2)}) collective-permute-start(bf16[4,128,768]{1,2,0:T(8,128)(2,1)} %copy.85), channel_id=1, source_target_pairs={{16,0},{20,4},{24,8},{28,12},{17,1},{21,5},{25,9},{29,13},{18,2},{... | collective-permute-start | bytes 2359304 | tf_op jit(solution)/shard_map/ppermute | solution.py:20
  333.7 60.5 %collective-permute-start.11 = (bf16[4,128,768]{1,2,0:T(8,128)(2,1)}, bf16[4,128,768]{1,2,0:T(8,128)(2,1)}, u32[]{:S(2)}, u32[]{:S(2)}) collective-permute-start(bf16[4,128,768]{1,2,0:T(8,128)(2,1)} %copy.85), channel_id=1, source_target_pairs={{20,0},{24,4},{28,8},{21,1},{25,5},{29,9},{22,2},{26,6},{30,10},{2... | collective-permute-start | bytes 2359304 | tf_op jit(solution)/shard_map/ppermute | solution.py:20
  338.3 9.9 copy-start.52
  338.3 10.5 copy-start.34
  381.9 29.1 %collective-permute-start.12 = (bf16[4,128,768]{1,2,0:T(8,128)(2,1)}, bf16[4,128,768]{1,2,0:T(8,128)(2,1)S(1)}, u32[]{:S(2)}, u32[]{:S(2)}) collective-permute-start(bf16[4,128,768]{1,2,0:T(8,128)(2,1)} %copy.85), channel_id=1, source_target_pairs={{24,0},{28,4},{25,1},{29,5},{26,2},{30,6},{27,3},{31,7}} | collective-permute-start | bytes 2359304 | tf_op jit(solution)/shard_map/ppermute | solution.py:20
  384.4 43.4 %collective-permute-start.13 = (bf16[4,128,768]{1,2,0:T(8,128)(2,1)}, bf16[4,128,768]{1,2,0:T(8,128)(2,1)S(1)}, u32[]{:S(2)}, u32[]{:S(2)}) collective-permute-start(bf16[4,128,768]{1,2,0:T(8,128)(2,1)} %copy.85), channel_id=1, source_target_pairs={{28,0},{29,1},{30,2},{31,3}} | collective-permute-start | bytes 2359304 | tf_op jit(solution)/shard_map/ppermute | solution.py:20
  432.2 6.5 copy-start.12
  432.2 6.5 copy-start.13
  451.9 6.5 copy-start.12
  451.9 6.5 copy-start.13
  471.6 6.5 copy-start.12
  471.6 6.5 copy-start.13
  491.4 6.5 copy-start.12
  491.4 6.5 copy-start.13
  511.1 6.5 copy-start.12
  511.1 6.5 copy-start.13
  530.9 6.5 copy-start.12
  588.3 7.9 copy-start.99
  596.2 17.6 %slice-start = ((s8[5505024]{0:T(1024)(128)(4,1)}), s8[4194304]{0:T(1024)(128)(4,1)S(1)}, s32[]{:S(2)}) async-start(s8[5505024]{0:T(1024)(128)(4,1)} %bitcast.419), calls=%async_computation.1 | async-start | bytes 8388608
  596.2 17.6 %slice-start.1 = ((s8[5505024]{0:T(1024)(128)(4,1)}), s8[1310720]{0:T(1024)(128)(4,1)S(1)}, s32[]{:S(2)}) async-start(s8[5505024]{0:T(1024)(128)(4,1)} %bitcast.419), calls=%async_computation.2 | async-start | bytes 2621440
  596.2 17.6 %copy-start.58 = (f32[256,768]{0,1:T(8,128)S(1)}, f32[256,768]{0,1:T(8,128)}, u32[]{:S(2)}) copy-start(f32[256,768]{0,1:T(8,128)} %get-tuple-element.151) | copy-start | bytes 2359300
  665.5 7.6 copy-start.94
  1384.9 9.4 copy-start.93
  1384.9 9.4 copy-start.25
  1384.9 9.4 copy-start.29
  1384.9 9.4 copy-start.40
  1385.0 9.4 copy-start.62
  1385.0 9.4 copy-start.89
  1730.9 9.1 copy-start.71
  1730.9 9.1 copy-start.73
  1730.9 9.1 copy-start.82
  (158 other events, 498.6 us)
Sparse Core Ops, SparseCore 0:
  1385.0 286.8 all-reduce.8
where the time goes:
time: 1780 us; the launch traced here: 1760 us
  blocking collectives  592 us (33%)
  local copies, waits for them, and re-layouts  409 us (23%)
  waiting for transfers between devices  348 us (20%)
  matrix products  336 us (19%)
  other arithmetic  30.5 us (2%)
  starting transfers between devices  22.9 us (1%)
    unnamed x1, blocking collectives  592 us
    unnamed x2, waiting for transfers between devices  276 us
    unnamed x214, local copies, waits for them, and re-layouts  152 us
    dot_general x32, matrix products, apply_split(): jnp.einsum(pattern, halves[1], values, preferred_element_type=jnp.float32)  105 us
    ppermute x14, waiting for transfers between devices, shifted(): return lax.ppermute(value, axis, pairs)  72 us
    dot_general x32, matrix products, apply_split(): jnp.einsum(pattern, halves[0], values, preferred_element_type=jnp.float32)  56.4 us
    slice x9, local copies, waits for them, and re-layouts, sum_everywhere(): results.append(summed[offset:offset + piece.size].reshape(piece.shape))  53.7 us
    while x224, local copies, waits for them, and re-layouts  46.7 us
  transfers between devices with their start and end apart: 15, of which 6 were waited for; matrix products, arithmetic and copies ran while one was open for 10% of the time, Pallas kernels for 0%

commit v1 on v0

--- a/solution.py
+++ b/solution.py
@@ -2,16 +2,415 @@
 
 import jax
 import jax.numpy as jnp
+import numpy as np
 from jax import lax
+from jax.experimental import pallas as pl
+from jax.experimental.pallas import tpu as pltpu
 from jax.sharding import PartitionSpec as P
 
-KL = 2048
-BANDS = 16
-LAGS = 16
-
-
+AX = ("seq", "dp")
 HIGH = lax.Precision.HIGHEST
 EPSILON = 1e-05
+BANDS = 16
+KL = 2048
+F32 = jnp.float32
+BF16 = jnp.bfloat16
+
+
+def mm(a, b, ca=1, cb=0):
+    return lax.dot_general(a, b, (((ca,), (cb,)), ((), ())), preferred_element_type=F32)
+
+
+def perm_of(f):
+    pairs = []
+    for z in range(4):
+        for x in range(2):
+            for y in range(2):
+                for c in range(2):
+                    a, b, d, e = f(z, x, y, c)
+                    pairs.append(((z * 2 + x) * 4 + y * 2 + c, (a * 2 + b) * 4 + d * 2 + e))
+    return pairs
+
+
+PC = perm_of(lambda z, x, y, c: (z, x, y, 1 - c))
+PX = perm_of(lambda z, x, y, c: (z, 1 - x, y, c))
+PY = perm_of(lambda z, x, y, c: (z, x, 1 - y, c))
+PZ = [perm_of(lambda z, x, y, c, k=k: (z ^ k, x, y, c)) for k in range(4)]
+
+
+def send(v, perm):
+    return lax.ppermute(v, AX, perm)
+
+
+def tie(*vals):
+    return lax.optimization_barrier(tuple(vals))
+
+
+def swap_in(v, c):
+    v = v.reshape(4, 2, 64, v.shape[-1])
+    keep = pick(v, c, 1)
+    got = send(pick(v, 1 - c, 1), PC)
+    return jnp.where(c == 0, jnp.concatenate([keep, got]), jnp.concatenate([got, keep]))
+
+
+def exchange_seq(v):
+    return lax.all_to_all(v, "seq", 0, 0)
+
+
+def swap_out(v, c):
+    v = v.reshape(2, 4, 64, v.shape[-1])
+    keep = pick(v, c)
+    got = send(pick(v, 1 - c), PC)
+    m = jnp.stack([jnp.where(c == 0, keep, got), jnp.where(c == 0, got, keep)], axis=1)
+    return m.reshape(4, 128, v.shape[-1])
+
+
+def both(own, c):
+    other = send(own, PC)
+    return jnp.stack([jnp.where(c == 0, own, other), jnp.where(c == 0, other, own)], axis=1)
+
+
+def feature_table(taps):
+    steps = np.arange(taps, dtype=np.float64) / KL
+    freqs = np.arange(1, BANDS + 1, dtype=np.float64)
+    phase = 2.0 * math.pi * steps[:, None] * freqs[None, :]
+    return np.concatenate([steps[:, None], np.cos(phase), np.sin(phase)], axis=1).astype(np.float32)
+
+
+def dft_table(length):
+    f = 2 * np.arange(length, dtype=np.int64)[:, None] + 1
+    n = np.arange(length, dtype=np.int64)[None, :]
+    angle = (f * n % (4 * length)) * (2.0 * math.pi / (4 * length))
+    return np.concatenate([np.cos(angle), -np.sin(angle)], axis=0).astype(np.float32)
+
+
+def norm_parts(v):
+    center = v - jnp.mean(v, axis=-1, keepdims=True)
+    spread_ = jnp.mean(center * center, axis=-1, keepdims=True)
+    inv = lax.rsqrt(spread_ + EPSILON)
+    return center * inv, inv
+
+
+def norm_back(q, hat, inv):
+    return (q - jnp.mean(q, -1, keepdims=True) - hat * jnp.mean(q * hat, -1, keepdims=True)) * inv
+
+
+def lanes(a, at, size):
+    return lax.dynamic_slice_in_dim(a, at, size, axis=1)
+
+
+def in_order(bit, own, other, axis=0):
+    first = jnp.where(bit == 0, own, other)
+    second = jnp.where(bit == 0, other, own)
+    return jnp.concatenate([first, second], axis=axis)
+
+
+def pick(a, i, axis=0):
+    return lax.dynamic_index_in_dim(a, i, axis, keepdims=False)
+
+
+class Reducer:
+    def __init__(self, sends, keeps, z, x, y):
+        self.pos, self.z0, self.z1 = (x, y), z & 1, z >> 1
+        self.sends, self.keeps = sends, keeps
+        self.cols = keeps[0].shape[1]
+        self.r = keeps[0].shape[0] // 8
+
+    def start1(self):
+        self.got = (send(self.sends[0], PX), send(self.sends[1], PY))
+
+    def start2(self):
+        pos = self.pos[::-1]
+        sums = [k + g.astype(F32) for k, g in zip(self.keeps, self.got)]
+        sums = [s.reshape(2, 4 * self.r, self.cols) for s in sums]
+        self.keeps = [pick(s, p) for s, p in zip(sums, pos)]
+        out = [pick(s, 1 - p).astype(BF16) for s, p in zip(sums, pos)]
+        self.got = (send(out[0], PY), send(out[1], PX))
+
+    def start3(self):
+        sums = [k + g.astype(F32) for k, g in zip(self.keeps, self.got)]
+        w = [s.reshape(2, 2 * self.r, self.cols) for s in sums]
+        self.keeps = jnp.stack([pick(v, self.z0) for v in w])
+        self.got = (send(jnp.stack([pick(v, 1 - self.z0).astype(BF16) for v in w]), PZ[1]),)
+
+    def start4(self):
+        w = self.keeps + self.got[0].astype(F32)
+        w = w.reshape(2, 2, self.r, self.cols)
+        self.keeps = pick(w, self.z1, 1)
+        self.got = (send(pick(w, 1 - self.z1, 1).astype(BF16), PZ[2]),)
+
+    def start5(self):
+        self.total = (self.keeps + self.got[0].astype(F32)).astype(BF16)
+        self.got = (send(self.total, PZ[2]),)
+
+    def start6(self):
+        self.total = in_order(self.z1, self.total, self.got[0], 1)
+        self.got = (send(self.total, PZ[1]),)
+
+    def start7(self):
+        v = in_order(self.z0, self.total, self.got[0], 1)
+        self.own = [v[0], v[1]]
+        self.got = (send(v[0], PY), send(v[1], PX))
+
+    def start8(self):
+        pos = self.pos[::-1]
+        self.near = [in_order(p, o, g) for p, o, g in zip(pos, self.own, self.got)]
+        self.got = (send(self.near[0], PX), send(self.near[1], PY))
+        self.pair_near = [send(v, PC) for v in self.near]
+
+    def start9(self):
+        self.far = list(self.got)
+        self.pair_far = [send(v, PC) for v in self.far]
+
+
+def write(bufs, sources, spots, moves):
+    n, m = len(sources), len(bufs)
+    rows, cols = sources[0].shape
+    each = len(moves(0, [0] * spots.shape[1]))
+
+    def body(*refs):
+        spot = refs[0]
+        src, out, wide, sem = refs[1 : 1 + n], refs[1 + n + m : 1 + n + 2 * m], refs[-2], refs[-1]
+        copies = []
+        for k in range(n):
+            wide[k] = src[k][...].astype(F32)
+            for q, (b, i, j, at, size) in enumerate(moves(k, [spot[k, e] for e in range(spots.shape[1])])):
+                copy = pltpu.make_async_copy(
+                    wide.at[k, :, pl.ds(at, size)],
+                    out[b].at[pl.ds(pl.multiple_of(i, 8), rows), pl.ds(pl.multiple_of(j, 128), size)],
+                    sem.at[k, q],
+                )
+                copy.start()
+                copies.append(copy)
+        for copy in copies:
+            copy.wait()
+
+    return pl.pallas_call(
+        body,
+        in_specs=[pl.BlockSpec(memory_space=pltpu.SMEM)]
+        + [pl.BlockSpec(memory_space=pltpu.VMEM)] * n
+        + [pl.BlockSpec(memory_space=pl.ANY)] * m,
+        out_specs=[pl.BlockSpec(memory_space=pl.ANY)] * m,
+        out_shape=[jax.ShapeDtypeStruct(b.shape, F32) for b in bufs],
+        input_output_aliases={1 + n + b: b for b in range(m)},
+        scratch_shapes=[pltpu.VMEM((n, rows, cols), F32), pltpu.SemaphoreType.DMA((n, each))],
+        compiler_params=pltpu.CompilerParams(vmem_limit_bytes=32 * 2**20),
+    )(spots, *sources, *bufs)
+
+
+def fresh(*shapes):
+    def body(*refs):
+        pass
+
+    return pl.pallas_call(
+        body,
+        out_specs=[pl.BlockSpec(memory_space=pl.ANY)] * len(shapes),
+        out_shape=[jax.ShapeDtypeStruct(s, F32) for s in shapes],
+    )()
+
+
+def write_down(k, s):
+    return [(0, s[0] * 1536 + s[1] * 768 + s[2] * 384, 0, 0, 768)]
+
+
+def write_up(k, s):
+    return [(0, s[1] * 384 + s[2] * 192, s[0] * 1536, 0, 1536)]
+
+
+def write_mix(k, s):
+    moves = [(0, s[1] * 384 + s[2] * 192, g * 768 + s[0] * 384, g * 384, 384) for g in range(3)]
+    return moves + [(1, s[0] * 384 + s[2] * 192, s[1] * 384, 1152, 384)]
+
+
+def hold(reducer, *vals):
+    n = len(reducer.got)
+    out = tie(*reducer.got, *vals)
+    reducer.got = tuple(out[:n])
+    return out[n] if len(vals) == 1 else out[n:]
+
+
+GELU_A = math.sqrt(2.0 / math.pi)
+GELU_B = 0.044715
+
+
+def gelu_pair(v):
+    sq = v * v
+    t = jnp.tanh(GELU_A * v * (1.0 + GELU_B * sq))
+    up = 0.5 * (1.0 + t)
+    return v * up, up + 0.5 * v * (1.0 - t * t) * (GELU_A * (1.0 + 3.0 * GELU_B * sq))
+
+
+def chip_local(
+    inputs, lengths, norm_gain, norm_bias, mixer_in, filter_in, filter_in_bias, filter_mid, filter_mid_bias,
+    filter_out, mixer_out, second_gain, second_bias, up_weight, down_weight, cotangent,
+):
+    s = lax.axis_index("seq")
+    d = lax.axis_index("dp")
+    z, x, y, c = s // 2, s % 2, d // 2, d % 2
+    width = inputs.shape[-1]
+    rows = 8 * inputs.shape[1]
+    half = width // 2
+    ff = up_weight.shape[1] // 2
+    x_half = exchange_seq(swap_in(inputs, c))
+    other_len = send(lengths, PC)
+    length = pick(jnp.where(c == (z >> 1), lengths, other_len), (z & 1) * 2 + x)
+    valid = (jnp.arange(rows, dtype=jnp.int32) < length).astype(F32)[:, None]
+    cot_half = swap_in(cotangent, c)
+    zero = 0 * c
+    near = jnp.stack([jnp.stack(v) for v in ((c, zero, x), (c, zero + 1, y), (1 - c, zero, x), (1 - c, zero + 1, y))])
+    far = jnp.stack(
+        [jnp.stack(v) for v in ((c, zero, 1 - x), (c, zero + 1, 1 - y), (1 - c, zero, 1 - x), (1 - c, zero + 1, 1 - y))]
+    )
+    w_in = jnp.concatenate([lanes(mixer_in, g * width + c * half, half) for g in range(3)], axis=1)
+    w_mo = lax.dynamic_slice_in_dim(mixer_out, c * half, half, 0)
+    w_up = lanes(up_weight, c * ff, ff)
+    w_dn = lax.dynamic_slice_in_dim(down_weight, c * ff, ff, 0)
+    f_out = lanes(filter_out, c * half, half)
+    table = jnp.asarray(dft_table(rows), BF16)
+    feats = jnp.asarray(feature_table(rows))
+    first_act = jnp.dot(feats, filter_in, precision=HIGH) + filter_in_bias
+    h1 = jnp.sin(first_act)
+    second_act = jnp.dot(h1, filter_mid, precision=HIGH) + filter_mid_bias
+    h2 = jnp.sin(second_act)
+    h2_hi = h2.astype(BF16)
+    h2_lo = (h2 - h2_hi.astype(F32)).astype(BF16)
+    hf = mm(table, jnp.concatenate([h2_hi, h2_lo], axis=1))
+    hf = (hf[:, :64] + hf[:, 64:]) * (1.0 / rows)
+    k = jnp.dot(hf, f_out, precision=HIGH)
+    x_half, k, w_in, w_mo, w_up, w_dn, cot_half, valid, near, far = tie(
+        x_half, k, w_in, w_mo, w_up, w_dn, cot_half, valid, near, far
+    )
+    cot_half = exchange_seq(cot_half)
+    k_re, k_im = k[:rows], k[rows:]
+    x_full = both(x_half, c).reshape(rows, width)
+    xf = x_full.astype(F32)
+    hat1, inv1 = norm_parts(xf)
+    normed = (hat1 * norm_gain + norm_bias).astype(BF16)
+    proj = mm(normed, w_in)
+    value, gate_a, gate_b = proj[:, :half], proj[:, half : 2 * half], proj[:, 2 * half :]
+    gated = (value * gate_a).astype(BF16) * valid.astype(BF16)
+    zf = mm(table, gated)
+    z_re, z_im = zf[:rows], zf[rows:]
+    yf = jnp.concatenate([k_re * z_re - k_im * z_im, k_re * z_im + k_im * z_re]).astype(BF16)
+    mixed = mm(table, yf, 0, 0)
+    gated_out = (gate_b * mixed).astype(BF16)
+    part = mm(gated_out, w_mo)
+    middle = xf + part + send(part.astype(BF16), PC).astype(F32)
+    hat2, inv2 = norm_parts(middle)
+    second_normed = (hat2 * second_gain + second_bias).astype(BF16)
+    activated, dgelu = gelu_pair(mm(second_normed, w_up))
+    activated, dgelu = activated.astype(BF16), dgelu.astype(BF16)
+    cot = both(cot_half, c).reshape(rows, width)
+    g_down = mm(activated, cot, 0, 0).reshape(2, 2, ff // 4, width)
+    down = Reducer(
+        [pick(g_down[0], 1 - x).astype(BF16), pick(g_down[1], 1 - y).astype(BF16)],
+        [pick(g_down[0], x), pick(g_down[1], y)], z, x, y,
+    )
+    down.start1()
+    d_pre = (mm(cot, w_dn, 1, 1) * dgelu.astype(F32)).astype(BF16)
+    g_up = mm(second_normed, d_pre, 0, 0).reshape(2, 2, half // 2, ff)
+    up = Reducer(
+        [pick(g_up[0], 1 - x).astype(BF16), pick(g_up[1], 1 - y).astype(BF16)],
+        [pick(g_up[0], x), pick(g_up[1], y)], z, x, y,
+    )
+    up.start1()
+    d_second_part = mm(d_pre, w_up, 1, 1)
+    d_second_part = hold(down, d_second_part)
+    down.start2()
+    g_second_bias = jnp.sum(d_second_part, axis=0)
+    g_second_gain = jnp.sum(d_second_part * hat2, axis=0)
+    d_second = d_second_part + send(d_second_part.astype(BF16), PC).astype(F32)
+    d_middle = cot.astype(F32) + norm_back(d_second * second_gain, hat2, inv2)
+    d_middle_low = d_middle.astype(BF16)
+    d_go = mm(d_middle_low, w_mo, 1, 1)
+    d_gate_b = (d_go * mixed).astype(BF16)
+    d_mixed = (d_go * gate_b).astype(BF16)
+    d_mixed = hold(up, d_mixed)
+    up.start2()
+    df = mm(table, d_mixed)
+    d_re, d_im = df[:rows], df[rows:]
+    gf = jnp.concatenate([k_re * d_re + k_im * d_im, k_re * d_im - k_im * d_re]).astype(BF16)
+    gf = hold(down, gf)
+    down.start3()
+    d_gated = mm(table, gf, 0, 0) * valid
+    d_proj = jnp.concatenate([(d_gated * gate_a).astype(BF16), (d_gated * value).astype(BF16), d_gate_b], axis=1)
+    g_in = mm(normed, d_proj, 0, 0).reshape(2, 2, half // 2, 3 * half)
+    g_mo = mm(gated_out, d_middle_low, 0, 0)
+    g_mo = [g_mo[:, :half].reshape(2, half // 2, half), g_mo[:, half:].reshape(2, half // 2, half)]
+
+    def mix_part(n, i):
+        return jnp.concatenate([pick(g_in[n], i), pick(g_mo[n], i)], axis=1)
+
+    mix = Reducer(
+        [mix_part(0, 1 - x).astype(BF16), mix_part(1, 1 - y).astype(BF16)],
+        [mix_part(0, x), mix_part(1, y)], z, x, y,
+    )
+    mix.start1()
+    d_proj = hold(up, d_proj)
+    up.start3()
+    d_proj = hold(down, d_proj)
+    down.start4()
+    d_normed_part = mm(d_proj, w_in, 1, 1)
+    d_normed_part = hold(down, d_normed_part)
+    down.start5()
+    d_normed_part = hold(up, d_normed_part)
+    up.start4()
+    g_norm_bias = jnp.sum(d_normed_part, axis=0)
+    g_norm_gain = jnp.sum(d_normed_part * hat1, axis=0)
+    dn = d_normed_part.reshape(8, 2, 64, width)
+    dn_own = pick(dn, c, 1) + send(pick(dn, 1 - c, 1).astype(BF16), PC).astype(F32)
+    hat1_own = pick(hat1.reshape(8, 2, 64, width), c, 1)
+    inv1_own = pick(inv1.reshape(8, 2, 64, 1), c, 1)
+    dx = pick(d_middle.reshape(8, 2, 64, width), c, 1) + norm_back(dn_own * norm_gain, hat1_own, inv1_own)
+    out_part = mm(activated, w_dn).reshape(8, 2, 64, width)
+    middle_own = pick(middle.reshape(8, 2, 64, width), c, 1)
+    out_own = middle_own + pick(out_part, c, 1) + send(pick(out_part, 1 - c, 1).astype(BF16), PC).astype(F32)
+    back = jnp.concatenate([out_own.astype(BF16), dx.astype(BF16)], axis=2)
+    back = swap_out(exchange_seq(back), c)
+    output, grad_inputs = back[..., :width], back[..., width:].astype(F32)
+    tf = jnp.concatenate([z_re * d_re + z_im * d_im, z_re * d_im - z_im * d_re]) * (1.0 / rows)
+    tf_low = tf.astype(BF16)
+    g_fo = mm(hf.astype(BF16), tf_low, 0, 0) * rows
+    kf = mm(tf_low, f_out.astype(BF16), 1, 1)
+    d_h2 = mm(table, kf.astype(BF16), 0, 0)
+    d_s = jnp.cos(second_act) * d_h2
+    g_fm = jnp.dot(h1.T, d_s, precision=HIGH)
+    g_fmb = jnp.sum(d_s, axis=0)
+    d_f = jnp.cos(first_act) * jnp.dot(d_s, filter_mid.T, precision=HIGH)
+    g_fi = jnp.dot(feats.T, d_f, precision=HIGH)
+    g_fib = jnp.sum(d_f, axis=0)
+    zero = jnp.zeros_like(g_fo)
+    g_fo_full = jnp.concatenate([jnp.where(c == 0, g_fo, zero), jnp.where(c == 0, zero, g_fo)], axis=1)
+    misc = jnp.concatenate([g_fm, g_fi, g_fmb[None], g_fib[None]])
+    misc = jnp.pad(misc, ((0, 104 - misc.shape[0]), (0, 0)))
+    misc = jnp.concatenate([misc[i * 8 : (i + 1) * 8] for i in range(13)], axis=1)
+    misc = jnp.concatenate([misc[:, :416], misc[:, 416:]])
+    misc = jnp.pad(misc, ((0, 0), (0, width - 416)))
+    vecs = jnp.stack([g_norm_gain, g_norm_bias, g_second_gain, g_second_bias])
+    vecs = jnp.pad(vecs, ((0, 4), (0, 0)))
+    small = jnp.concatenate([g_fo_full, misc, vecs])
+    for perm in (PC, PX, PY, PZ[1], PZ[2]):
+        small = small + send(small, perm)
+    misc = jnp.concatenate([small[64:72, :416], small[72:80, :416]], axis=1)
+    misc = jnp.concatenate([misc[:, i * 64 : (i + 1) * 64] for i in range(13)])
+    vecs = small[80:84]
+    bufs = fresh(down_weight.shape, up_weight.shape, mixer_in.shape, mixer_out.shape)
+    outs = []
+    for reducer, first, mine, moves in (
+        (down, 6, bufs[:1], write_down), (up, 5, bufs[1:2], write_up), (mix, 2, bufs[2:], write_mix),
+    ):
+        for n in range(first, 10):
+            getattr(reducer, f"start{n}")()
+        mine = write(mine, reducer.near + reducer.pair_near, near, moves)
+        outs += write(mine, reducer.far + reducer.pair_far, far, moves)
+    grad_down, grad_up, grad_in, grad_mo = outs
+    return (
+        output, grad_inputs, vecs[0], vecs[1], grad_in, misc[64:97], misc[98], misc[:64], misc[97],
+        small[:64], grad_mo, vecs[2], vecs[3], grad_up, grad_down,
+    )
+
+
+LAGS = 16
 
 
 def shifted(value, axis, by):
@@ -20,27 +419,27 @@
     return lax.ppermute(value, axis, pairs)
 
 
-def layer_norm(values, gain, shift):
+def plain_norm(values, gain, shift):
     center = values - jnp.mean(values, axis=-1, keepdims=True)
     spread = jnp.mean(center * center, axis=-1, keepdims=True)
     return center * lax.rsqrt(spread + EPSILON) * gain + shift
 
 
-def feature_table(taps, bands):
+def features_of(taps, bands):
     steps = jnp.arange(taps, dtype=jnp.float32) / taps
     freqs = jnp.arange(1, bands + 1, dtype=jnp.float32)
     phase = 2.0 * math.pi * steps[:, None] * freqs[None, :]
     return jnp.concatenate([steps[:, None], jnp.cos(phase), jnp.sin(phase)], axis=1)
 
 
-def filter_kernel(filter_in, filter_in_bias, filter_mid, filter_mid_bias, filter_out):
-    table = feature_table(KL, BANDS)
+def taps_of(filter_in, filter_in_bias, filter_mid, filter_mid_bias, filter_out):
+    table = features_of(KL, BANDS)
     first = jnp.sin(jnp.dot(table, filter_in, precision=HIGH) + filter_in_bias)
     second = jnp.sin(jnp.dot(first, filter_mid, precision=HIGH) + filter_mid_bias)
     return jnp.dot(second, filter_out, precision=HIGH)
 
 
-def dft_tables(block_len):
+def wave_tables(block_len):
     length = 2 * block_len
     index = jnp.arange(length, dtype=jnp.int32)
     angle = (index[:, None] * index[None, :] % length).astype(jnp.float32) * (
@@ -163,7 +562,7 @@
     return results
 
 
-def local(
+def block_local(
     inputs,
     lengths,
     norm_gain,
@@ -187,14 +586,14 @@
     rank = lax.axis_index("seq")
     position = rank * block_len + jnp.arange(block_len, dtype=jnp.int32)
     valid = (position[None, :] < lengths[:, None]).astype(jnp.float32)[:, :, None]
-    cos_t, sin_t = dft_tables(block_len)
+    cos_t, sin_t = wave_tables(block_len)
     tables = low_tables(cos_t, sin_t)
     kernel, filter_back = jax.vjp(
-        filter_kernel, filter_in, filter_in_bias, filter_mid, filter_mid_bias, filter_out
+        taps_of, filter_in, filter_in_bias, filter_mid, filter_mid_bias, filter_out
     )
     k_real, k_imag = kernel_freq(kernel, cos_t, sin_t)
     x_full = inputs.astype(jnp.float32).reshape(row_count, width)
-    normed = layer_norm(x_full, norm_gain, norm_bias).astype(jnp.bfloat16)
+    normed = plain_norm(x_full, norm_gain, norm_bias).astype(jnp.bfloat16)
     projected = jnp.dot(normed, mixer_in, preferred_element_type=jnp.float32)
     value = projected[:, :width]
     gate_a = projected[:, width : 2 * width]
@@ -216,7 +615,7 @@
     mixed = from_freq(y_real, y_imag, cos_t, sin_t).reshape(row_count, width)
     gated_out = (gate_b * mixed).astype(jnp.bfloat16)
     middle = x_full + jnp.dot(gated_out, mixer_out, preferred_element_type=jnp.float32)
-    second_normed = layer_norm(middle, second_gain, second_bias).astype(jnp.bfloat16)
+    second_normed = plain_norm(middle, second_gain, second_bias).astype(jnp.bfloat16)
     pre = jnp.dot(second_normed, up_weight, preferred_element_type=jnp.float32)
     activated = jax.nn.gelu(pre, approximate=True).astype(jnp.bfloat16)
     result = middle + jnp.dot(activated, down_weight, preferred_element_type=jnp.float32)
@@ -229,7 +628,7 @@
     d_pre = gelu_back(d_act)[0].astype(jnp.bfloat16)
     grad_up = jnp.einsum("rd,rk->dk", second_normed, d_pre, preferred_element_type=jnp.float32)
     d_second = jnp.einsum("rk,dk->rd", d_pre, up_weight, preferred_element_type=jnp.float32)
-    _, second_back = jax.vjp(layer_norm, middle, second_gain, second_bias)
+    _, second_back = jax.vjp(plain_norm, middle, second_gain, second_bias)
     d_middle_norm, grad_second_gain, grad_second_bias = second_back(d_second)
     d_middle = upstream + d_middle_norm
     d_middle_low = d_middle.astype(jnp.bfloat16)
@@ -266,7 +665,7 @@
     )
     grad_mixer_in = jnp.einsum("rd,rk->dk", normed, d_projected, preferred_element_type=jnp.float32)
     d_normed = jnp.einsum("rk,dk->rd", d_projected, mixer_in, preferred_element_type=jnp.float32)
-    _, first_back = jax.vjp(layer_norm, x_full, norm_gain, norm_bias)
+    _, first_back = jax.vjp(plain_norm, x_full, norm_gain, norm_bias)
     d_x_norm, grad_norm_gain, grad_norm_bias = first_back(d_normed)
     grad_inputs = (d_middle + d_x_norm).reshape(seqs, block_len, width)
     _, kernel_back = jax.vjp(lambda kern: kernel_freq(kern, cos_t, sin_t), kernel)
@@ -303,40 +702,10 @@
     )
 
 
+SPECS_IN = (P("dp", "seq", None), P("dp")) + (P(),) * 13 + (P("dp", "seq", None),)
+SPECS_OUT = (P("dp", "seq", None), P("dp", "seq", None)) + (P(),) * 13
+
+
 def solution(mesh):
-    in_specs = (
-        P("dp", "seq", None),
-        P("dp"),
-        P(),
-        P(),
-        P(),
-        P(),
-        P(),
-        P(),
-        P(),
-        P(),
-        P(),
-        P(),
-        P(),
-        P(),
-        P(),
-        P("dp", "seq", None),
-    )
-    out_specs = (
-        P("dp", "seq", None),
-        P("dp", "seq", None),
-        P(),
-        P(),
-        P(),
-        P(),
-        P(),
-        P(),
-        P(),
-        P(),
-        P(),
-        P(),
-        P(),
-        P(),
-        P(),
-    )
-    return jax.shard_map(local, mesh=mesh, in_specs=in_specs, out_specs=out_specs, check_vma=False)
+    local = chip_local if (mesh.shape["seq"], mesh.shape["dp"]) == (8, 4) else block_local
+    return jax.shard_map(local, mesh=mesh, in_specs=SPECS_IN, out_specs=SPECS_OUT, check_vma=False)

time: 1780 us -> 417 us (0.23); the launches traced: 1760 us -> 412 us
  blocking collectives: 592 us -> 0 us
  local copies, waits for them, and re-layouts: 409 us -> 58.5 us
  matrix products: 336 us -> 85.7 us
  waiting for transfers between devices: 348 us -> 114 us
  starting transfers between devices: 22.9 us -> 79.2 us
  other arithmetic: 30.5 us -> 52 us
  Pallas kernels: 0 us -> 20.1 us
    unnamed x1 -> x0, blocking collectives: 592 us -> none
    unnamed x2 -> x0, waiting for transfers between devices: 276 us -> none
    dot_general x92 -> x26, matrix products: 336 us -> 85.7 us  [the longest x20 71.7 us: mm(): lax.dot_general(a, b, (((ca,), (cb,)), ((), ())), preferred_element_type=...]
    unnamed x214 -> x168, local copies, waits for them, and re-layouts: 152 us -> 18.4 us
    slice x13 -> x8, local copies, waits for them, and re-layouts: 79.4 us -> 6.01 us  [the longest x1 1.62 us: chip_local(): small[:64]]
    while x224 -> x0, local copies, waits for them, and re-layouts: 46.7 us -> none
    reshape x7 -> x0, local copies, waits for them, and re-layouts: 41.5 us -> none  [the longest x4 28.7 us: sum_everywhere(): flat_grads = jnp.concatenate([piece.reshape(-1) for piece in parts])]
    ppermute x14 -> x63, waiting for transfers between devices: 72 us -> 108 us  [send(): return lax.ppermute(v, AX, perm)]
  transfers between devices with their start and end apart: 15 -> 66, of which waited for: 6 -> 19; matrix products, arithmetic and copies ran while one was open for 10% -> 31% of each run, Pallas kernels for 0% -> 5%
where the time goes in v1:
time: 417 us; the launch traced here: 412 us
  waiting for transfers between devices  114 us (27%)
  matrix products  85.7 us (21%)
  starting transfers between devices  79.2 us (19%)
  local copies, waits for them, and re-layouts  58.5 us (14%)
  other arithmetic  52 us (12%)
  Pallas kernels  20.1 us (5%)
    ppermute x63, waiting for transfers between devices, send(): return lax.ppermute(v, AX, perm)  108 us
    dot_general x20, matrix products, mm(): lax.dot_general(a, b, (((ca,), (cb,)), ((), ())), preferred_element_type=...  71.7 us
    ppermute x63, starting transfers between devices, send(): return lax.ppermute(v, AX, perm)  58.5 us
    all_to_all x3, starting transfers between devices, exchange_seq(): return lax.all_to_all(v, 'seq', 0, 0)  20.7 us
    pallas_call x6, Pallas kernels, write(): pl.pallas_call(body, in_specs=[pl.BlockSpec(memory_space=pltpu.SMEM)] + [...  20.1 us
    unnamed x168, local copies, waits for them, and re-layouts  18.4 us
    squeeze x11, local copies, waits for them, and re-layouts, pick(): return lax.dynamic_index_in_dim(a, i, axis, keepdims=False)  13.4 us
  transfers between devices with their start and end apart: 66, of which 19 were waited for; matrix products, arithmetic and copies ran while one was open for 31% of the time, Pallas kernels for 5%

profile of v1, /device:TPU:31, one launch (start us, length us, event | category | flops | bytes accessed | tf_op | source)
XLA Modules:
  0.0 412.1 jit_solution(16364902361055607151)
XLA Ops:
  3.5 1.9 dynamic-slice_bitcast_fusion.4
  6.4 2.2 fusion.96
  9.3 1.9 fusion.97
  11.2 3.4 constant_dynamic-slice_fusion.8
  19.4 2.1 maximum_select_fusion
  21.5 5.4 %all-to-all-start = ((bf16[8,64,768]{2,1,0:T(8,128)(2,1)}), bf16[8,64,768]{2,1,0:T(8,128)(2,1)S(1)}, u32[]{:S(2)}, u32[]{:S(2)}) async-start(bf16[8,64,768]{2,1,0:T(8,128)(2,1)} %maximum_select_fusion), calls=%async_computation | async-start | bytes 1572864 | tf_op jit(solution)/shard_map/all_to_all | solution.py:57
  27.8 3.7 fusion.54
  32.5 4.3 %fusion.62 = f32[2048,384]{1,0:T(8,128)} fusion(f32[2048,128]{0,1:T(8,128)S(1)} %fusion.54, f32[64,768]{1,0:T(8,128)S(1)} %copy-done.63, s32[]{:T(128)S(6)} %select_n.323), kind=kOutput, calls=%fused_computation.222 | convolution fusion | flops 604241920 | bytes 4292612 | tf_op jit(solution)/shard_map/dot_general | solution.py:279
  39.2 6.3 %all-to-all-done = bf16[8,64,768]{2,1,0:T(8,128)(2,1)S(1)} async-done(((bf16[8,64,768]{2,1,0:T(8,128)(2,1)}), bf16[8,64,768]{2,1,0:T(8,128)(2,1)S(1)}, u32[]{:S(2)}, u32[]{:S(2)}) %all-to-all-start) | async-done | bytes 786464 | tf_op jit(solution)/shard_map/all_to_all | solution.py:57
  45.9 6.4 %all-to-all-start.1 = ((bf16[8,64,768]{2,1,0:T(8,128)(2,1)}), bf16[8,64,768]{2,1,0:T(8,128)(2,1)}, u32[]{:S(2)}, u32[]{:S(2)}) async-start(bf16[8,64,768]{2,1,0:T(8,128)(2,1)} %maximum_select_fusion.1), calls=%async_computation.1 | async-start | bytes 1572864 | tf_op jit(solution)/shard_map/all_to_all | solution.py:57
  54.7 2.2 broadcast_subtract_fusion
  57.0 2.2 copy.66
  61.1 2.2 fusion.103
  63.3 2.4 fusion.15
  70.3 2.5 fusion.9
  72.7 3.2 fusion.98
  77.1 3.8 collective-permute-done.6
  84.4 2.0 fusion.88
  88.1 15.5 %fusion.85 = f32[1024,1536]{1,0:T(8,128)S(1)} fusion(bf16[768,1536]{1,0:T(8,128)(2,1)S(1)} %copy-done.33, f32[1024,768]{1,0:T(8,128)S(1)} %get-tuple-element.100, f32[768]{0:T(1024)S(1)} %copy-done.79, f32[768]{0:T(1024)S(1)} %copy-done.66, f32[1024]{0:T(1024)S(1)} %add_rsqrt_fusion.1, f32[1024]{0:T(1024)S(1)} %broadcast_multiply_fusion.5), kind=kOutput, calls=%fused_computation.310 | convolution fusion | flops 2419851264 | bytes 11810816 | tf_op jit(solution)/shard_map/dot_general | solution.py:21
  103.6 3.7 fusion.87
  107.3 6.4 %multiply_convert_fusion = bf16[1024,1536]{1,0:T(8,128)(2,1)} fusion(bf16[1024,768]{1,0:T(8,128)(2,1)S(1)} %bitcast.308, bf16[1536,768]{1,0:T(8,128)(2,1)S(1)} %copy-done.34, f32[1024,1536]{1,0:T(8,128)S(1)} %fusion.85), kind=kOutput, calls=%fused_computation | convolution fusion | flops 2447376384 | bytes 13369344 | tf_op jit(solution)/shard_map/dot_general | solution.py:21
  113.7 3.8 fusion.86
  119.7 3.1 fusion.84
  122.9 2.6 fusion.104
  125.5 7.1 %collective-permute-done.8 = bf16[384,768]{1,0:T(8,128)(2,1)S(1)} collective-permute-done((bf16[384,768]{1,0:T(8,128)(2,1)S(1)}, bf16[384,768]{1,0:T(8,128)(2,1)S(1)}, u32[]{:S(2)}, u32[]{:S(2)}) %collective-permute-start.8) | collective-permute-done | bytes 589856 | tf_op jit(solution)/shard_map/ppermute | solution.py:42
  139.4 2.5 multiply_reduce_fusion
  141.9 2.1 multiply_add_fusion
  147.0 2.6 fusion.10
  152.4 2.3 fusion.105
  155.2 2.0 multiply_add_fusion.1
  165.5 4.4 %fusion.5 = (bf16[1024,384]{1,0:T(8,128)(2,1)S(1)}, bf16[1024,384]{1,0:T(8,128)(2,1)S(1)}) fusion(f32[1024,1152]{1,0:T(8,128)} %copy-done.32, f32[1024]{0:T(1024)S(1)} %bitcast.353, bf16[2048,384]{1,0:T(8,128)(2,1)S(1)} %pad_maximum_fusion.3, bf16[2048,1024]{1,0:T(8,128)(2,1)S(1)} %copy-done.13), kind=kOutput, calls=%fused_computation.37 | convolution fusion | flops 1612578816 | bytes 10489856 | tf_op jit(solution)/shard_map/dot_general | solution.py:21
  169.9 2.3 fusion.83
  180.9 5.5 %fusion.100 = (f32[64]{0:T(128)S(1)}, f32[1024,64]{0,1:T(8,128)S(1)}) fusion(bf16[2048,1024]{1,0:T(8,128)(2,1)} %constant.258.clone, f32[64,768]{1,0:T(8,128)} %param.27, s32[]{:T(128)S(6)} %select_n.323, f32[1024,384]{1,0:T(8,128)} %copy-done.22, f32[1024,384]{1,0:T(8,128)} %copy-done.21, f32[1024,64]{0,1:T(8,128)} %get-tuple-element.200), kind=kOutput, calls=%fused_computation.324 | convolution fusion | flops 371720128 | bytes 7913732 | tf_op jit(solution)/shard_map/dot_general | solution.py:21
  187.7 2.2 fusion.99
  189.9 2.1 fusion.108
  205.5 2.1 collective-permute-done.17
  208.4 2.2 fusion.106
  210.7 3.7 collective-permute-done.18
  214.5 2.2 collective-permute-done.16
  217.7 8.2 %collective-permute-start.21 = (f32[88,768]{1,0:T(8,128)S(1)}, f32[88,768]{1,0:T(8,128)S(1)}, u32[]{:S(2)}, u32[]{:S(2)}) collective-permute-start(f32[88,768]{1,0:T(8,128)S(1)} %pad_maximum_fusion.23), channel_id=1, source_target_pairs={{0,1},{1,0},{2,3},{3,2},{4,5},{5,4},{6,7},{7,6},{8,9},{9,8},{10,11... | collective-permute-start | bytes 811016 | tf_op jit(solution)/shard_map/ppermute | solution.py:42
  226.2 2.7 collective-permute-start.19
  233.8 7.2 %collective-permute-done.43 = bf16[2,24,1536]{2,1,0:T(8,128)(2,1)S(1)} collective-permute-done((bf16[2,24,1536]{2,1,0:T(8,128)(2,1)S(1)}, bf16[2,24,1536]{2,1,0:T(8,128)(2,1)S(1)}, u32[]{:S(2)}, u32[]{:S(2)}) %collective-permute-start.43) | collective-permute-done | bytes 147488 | tf_op jit(solution)/shard_map/ppermute | solution.py:42
  244.4 3.1 collective-permute-done.22
  250.7 3.7 collective-permute-start.61
  255.9 2.1 collective-permute-start.31
  258.8 5.2 %collective-permute-done.31 = bf16[2,24,1536]{2,1,0:T(8,128)(2,1)S(1)} collective-permute-done((bf16[2,24,1536]{2,1,0:T(8,128)(2,1)S(1)}, bf16[2,24,1536]{2,1,0:T(8,128)(2,1)S(1)}, u32[]{:S(2)}, u32[]{:S(2)}) %collective-permute-start.31) | collective-permute-done | bytes 147488 | tf_op jit(solution)/shard_map/ppermute | solution.py:42
  267.7 8.8 %all-to-all-start.2 = ((bf16[8,64,1536]{2,1,0:T(8,128)(2,1)}), bf16[8,64,1536]{2,1,0:T(8,128)(2,1)}, u32[]{:S(2)}, u32[]{:S(2)}) async-start(bf16[8,64,1536]{2,1,0:T(8,128)(2,1)} %pad_maximum_fusion.4), calls=%async_computation.2 | async-start | bytes 3145728 | tf_op jit(solution)/shard_map/all_to_all | solution.py:57
  276.5 3.5 collective-permute-start.62
  283.9 34.2 %collective-permute-done.32 = bf16[2,24,1536]{2,1,0:T(8,128)(2,1)S(1)} collective-permute-done((bf16[2,24,1536]{2,1,0:T(8,128)(2,1)S(1)}, bf16[2,24,1536]{2,1,0:T(8,128)(2,1)S(1)}, u32[]{:S(2)}, u32[]{:S(2)}) %collective-permute-start.32) | collective-permute-done | bytes 147488 | tf_op jit(solution)/shard_map/ppermute | solution.py:42
  318.9 7.5 %collective-permute-done.33 = bf16[2,48,1536]{2,1,0:T(8,128)(2,1)S(1)} collective-permute-done((bf16[2,48,1536]{2,1,0:T(8,128)(2,1)S(1)}, bf16[2,48,1536]{2,1,0:T(8,128)(2,1)S(1)}, u32[]{:S(2)}, u32[]{:S(2)}) %collective-permute-start.33) | collective-permute-done | bytes 294944 | tf_op jit(solution)/shard_map/ppermute | solution.py:42
  327.9 3.4 shard_map.294.refs_5_
  331.3 10.1 %collective-permute-done.25 = f32[88,768]{1,0:T(8,128)S(1)} collective-permute-done((f32[88,768]{1,0:T(8,128)S(1)}, f32[88,768]{1,0:T(8,128)S(1)}, u32[]{:S(2)}, u32[]{:S(2)}) %collective-permute-start.25) | collective-permute-done | bytes 270368 | tf_op jit(solution)/shard_map/ppermute | solution.py:42
  344.7 4.7 %collective-permute-done.36 = bf16[96,1536]{1,0:T(8,128)(2,1)S(1)} collective-permute-done((bf16[96,1536]{1,0:T(8,128)(2,1)S(1)}, bf16[96,1536]{1,0:T(8,128)(2,1)S(1)}, u32[]{:S(2)}, u32[]{:S(2)}) %collective-permute-start.36) | collective-permute-done | bytes 294944 | tf_op jit(solution)/shard_map/ppermute | solution.py:42
  352.7 3.8 collective-permute-done.34
  356.5 4.2 %collective-permute-start.59 = (bf16[384,768]{1,0:T(8,128)(2,1)S(1)}, bf16[384,768]{1,0:T(8,128)(2,1)S(1)}, u32[]{:S(2)}, u32[]{:S(2)}) collective-permute-start(bf16[384,768]{1,0:T(8,128)(2,1)S(1)} %collective-permute-done.56.refs_1_), channel_id=1, source_target_pairs={{0,1},{1,0},{2,3},{3,2},{4,5},{5,4},{6,7},{7,6},{8,9},{9,8},{10,11... | collective-permute-start | bytes 1769480 | tf_op jit(solution)/shard_map/ppermute | solution.py:42
  362.4 6.9 %collective-permute-done.48.refs_2_ = bf16[192,1536]{1,0:T(8,128)(2,1)} collective-permute-done((bf16[192,1536]{1,0:T(8,128)(2,1)S(1)}, bf16[192,1536]{1,0:T(8,128)(2,1)}, u32[]{:S(2)}, u32[]{:S(2)}) %collective-permute-start.48) | collective-permute-done | bytes 589856 | tf_op jit(solution)/shard_map/ppermute | solution.py:42
  369.3 4.2 %collective-permute-start.49 = (bf16[192,1536]{1,0:T(8,128)(2,1)}, bf16[192,1536]{1,0:T(8,128)(2,1)}, u32[]{:S(2)}, u32[]{:S(2)}) collective-permute-start(bf16[192,1536]{1,0:T(8,128)(2,1)} %collective-permute-done.46.refs_1_), channel_id=1, source_target_pairs={{0,1},{1,0},{2,3},{3,2},{4,5},{5,4},{6,7},{7,6},{8,9},{9,8},{10,11... | collective-permute-start | bytes 1769480 | tf_op jit(solution)/shard_map/ppermute | solution.py:42
  378.3 3.6 collective-permute-done.37.refs_2_
  381.9 2.3 collective-permute-start.41
  392.0 2.9 shard_map.292.refs_5_
  394.9 3.4 shard_map.295
  398.2 3.9 shard_map.293
  402.2 3.0 shard_map.290
  405.1 3.6 shard_map.291
  (440 shorter events, 124.8 us)
Async XLA Ops:
  0.7 36.1 %collective-permute-start.2 = (s32[4]{0:T(128)}, s32[4]{0:T(128)S(1)}, u32[]{:S(2)}, u32[]{:S(2)}) collective-permute-start(s32[4]{0:T(128)} %param.19), channel_id=1, source_target_pairs={{0,1},{1,0},{2,3},{3,2},{4,5},{5,4},{6,7},{7,6},{8,9},{9,8},{10,11... | collective-permute-start | bytes 56 | tf_op jit(solution)/shard_map/ppermute | solution.py:42
  3.4 16.0 %collective-permute-start = (bf16[4,64,768]{2,1,0:T(8,128)(2,1)}, bf16[4,64,768]{2,1,0:T(8,128)(2,1)}, u32[]{:S(2)}, u32[]{:S(2)}) collective-permute-start(bf16[4,64,768]{2,1,0:T(8,128)(2,1)} %get-tuple-element.137), channel_id=1, source_target_pairs={{0,1},{1,0},{2,3},{3,2},{4,5},{5,4},{6,7},{7,6},{8,9},{9,8},{10,11... | collective-permute-start | bytes 1179656 | tf_op jit(solution)/shard_map/ppermute | solution.py:42
  5.5 32.7 %collective-permute-start.1 = (bf16[4,64,768]{2,1,0:T(8,128)(2,1)}, bf16[4,64,768]{2,1,0:T(8,128)(2,1)S(1)}, u32[]{:S(2)}, u32[]{:S(2)}) collective-permute-start(bf16[4,64,768]{2,1,0:T(8,128)(2,1)} %get-tuple-element.135), channel_id=1, source_target_pairs={{0,1},{1,0},{2,3},{3,2},{4,5},{5,4},{6,7},{7,6},{8,9},{9,8},{10,11... | collective-permute-start | bytes 1179656 | tf_op jit(solution)/shard_map/ppermute | solution.py:42
  21.5 24.0 %all-to-all-start = ((bf16[8,64,768]{2,1,0:T(8,128)(2,1)}), bf16[8,64,768]{2,1,0:T(8,128)(2,1)S(1)}, u32[]{:S(2)}, u32[]{:S(2)}) async-start(bf16[8,64,768]{2,1,0:T(8,128)(2,1)} %maximum_select_fusion), calls=%async_computation | async-start | bytes 1572864 | tf_op jit(solution)/shard_map/all_to_all | solution.py:57
  45.5 7.0 %collective-permute-start.3 = (bf16[8,64,768]{2,1,0:T(8,128)(2,1)S(1)}, bf16[8,64,768]{2,1,0:T(8,128)(2,1)S(1)}, u32[]{:S(2)}, u32[]{:S(2)}) collective-permute-start(bf16[8,64,768]{2,1,0:T(8,128)(2,1)S(1)} %all-to-all-done), channel_id=1, source_target_pairs={{0,1},{1,0},{2,3},{3,2},{4,5},{5,4},{6,7},{7,6},{8,9},{9,8},{10,11... | collective-permute-start | bytes 2359304 | tf_op jit(solution)/shard_map/ppermute | solution.py:42
  45.9 30.3 %all-to-all-start.1 = ((bf16[8,64,768]{2,1,0:T(8,128)(2,1)}), bf16[8,64,768]{2,1,0:T(8,128)(2,1)}, u32[]{:S(2)}, u32[]{:S(2)}) async-start(bf16[8,64,768]{2,1,0:T(8,128)(2,1)} %maximum_select_fusion.1), calls=%async_computation.1 | async-start | bytes 1572864 | tf_op jit(solution)/shard_map/all_to_all | solution.py:57
  76.0 6.6 %collective-permute-start.4 = (bf16[1024,768]{1,0:T(8,128)(2,1)}, bf16[1024,768]{1,0:T(8,128)(2,1)}, u32[]{:S(2)}, u32[]{:S(2)}) collective-permute-start(bf16[1024,768]{1,0:T(8,128)(2,1)} %get-tuple-element.203), channel_id=1, source_target_pairs={{0,1},{1,0},{2,3},{3,2},{4,5},{5,4},{6,7},{7,6},{8,9},{9,8},{10,11... | collective-permute-start | bytes 4718600 | tf_op jit(solution)/shard_map/ppermute | solution.py:42
  117.9 14.7 %collective-permute-start.8 = (bf16[384,768]{1,0:T(8,128)(2,1)S(1)}, bf16[384,768]{1,0:T(8,128)(2,1)S(1)}, u32[]{:S(2)}, u32[]{:S(2)}) collective-permute-start(bf16[384,768]{1,0:T(8,128)(2,1)S(1)} %fusion.27), channel_id=1, source_target_pairs={{0,2},{1,3},{2,0},{3,1},{4,6},{5,7},{6,4},{7,5},{8,10},{9,11},{10,... | collective-permute-start | bytes 1769480 | tf_op jit(solution)/shard_map/ppermute | solution.py:42
  118.2 14.4 %collective-permute-start.7 = (bf16[384,768]{1,0:T(8,128)(2,1)S(1)}, bf16[384,768]{1,0:T(8,128)(2,1)S(1)}, u32[]{:S(2)}, u32[]{:S(2)}) collective-permute-start(bf16[384,768]{1,0:T(8,128)(2,1)S(1)} %fusion.26), channel_id=1, source_target_pairs={{0,4},{1,5},{2,6},{3,7},{4,0},{5,1},{6,2},{7,3},{8,12},{9,13},{10,... | collective-permute-start | bytes 1769480 | tf_op jit(solution)/shard_map/ppermute | solution.py:42
  118.7 18.3 %collective-permute-start.5 = (bf16[8,64,768]{2,1,0:T(8,128)(2,1)S(1)}, bf16[8,64,768]{2,1,0:T(8,128)(2,1)S(1)}, u32[]{:S(2)}, u32[]{:S(2)}) collective-permute-start(bf16[8,64,768]{2,1,0:T(8,128)(2,1)S(1)} %fusion.17), channel_id=1, source_target_pairs={{0,1},{1,0},{2,3},{3,2},{4,5},{5,4},{6,7},{7,6},{8,9},{9,8},{10,11... | collective-permute-start | bytes 2359304 | tf_op jit(solution)/shard_map/ppermute | solution.py:42
  132.8 6.7 %collective-permute-start.9 = (bf16[1024,768]{1,0:T(8,128)(2,1)S(1)}, bf16[1024,768]{1,0:T(8,128)(2,1)S(1)}, u32[]{:S(2)}, u32[]{:S(2)}) collective-permute-start(bf16[1024,768]{1,0:T(8,128)(2,1)S(1)} %convert_element_type.328), channel_id=1, source_target_pairs={{0,1},{1,0},{2,3},{3,2},{4,5},{5,4},{6,7},{7,6},{8,9},{9,8},{10,11... | collective-permute-start | bytes 4718600 | tf_op jit(solution)/shard_map/ppermute | solution.py:42
  134.8 15.0 %collective-permute-start.11 = (bf16[192,1536]{1,0:T(8,128)(2,1)S(1)}, bf16[192,1536]{1,0:T(8,128)(2,1)S(1)}, u32[]{:S(2)}, u32[]{:S(2)}) collective-permute-start(bf16[192,1536]{1,0:T(8,128)(2,1)S(1)} %fusion.29), channel_id=1, source_target_pairs={{0,2},{1,3},{2,0},{3,1},{4,6},{5,7},{6,4},{7,5},{8,10},{9,11},{10,... | collective-permute-start | bytes 1769480 | tf_op jit(solution)/shard_map/ppermute | solution.py:42
  136.1 14.7 %collective-permute-start.10 = (bf16[192,1536]{1,0:T(8,128)(2,1)S(1)}, bf16[192,1536]{1,0:T(8,128)(2,1)S(1)}, u32[]{:S(2)}, u32[]{:S(2)}) collective-permute-start(bf16[192,1536]{1,0:T(8,128)(2,1)S(1)} %fusion.28), channel_id=1, source_target_pairs={{0,4},{1,5},{2,6},{3,7},{4,0},{5,1},{6,2},{7,3},{8,12},{9,13},{10,... | collective-permute-start | bytes 1769480 | tf_op jit(solution)/shard_map/ppermute | solution.py:42
  136.5 24.1 %collective-permute-start.14 = (bf16[192,768]{1,0:T(8,128)(2,1)S(1)}, bf16[192,768]{1,0:T(8,128)(2,1)}, u32[]{:S(2)}, u32[]{:S(2)}) collective-permute-start(bf16[192,768]{1,0:T(8,128)(2,1)S(1)} %fusion.37), channel_id=1, source_target_pairs={{0,2},{1,3},{2,0},{3,1},{4,6},{5,7},{6,4},{7,5},{8,10},{9,11},{10,... | collective-permute-start | bytes 884744 | tf_op jit(solution)/shard_map/ppermute | solution.py:42
  137.0 23.6 %collective-permute-start.15 = (bf16[192,768]{1,0:T(8,128)(2,1)S(1)}, bf16[192,768]{1,0:T(8,128)(2,1)}, u32[]{:S(2)}, u32[]{:S(2)}) collective-permute-start(bf16[192,768]{1,0:T(8,128)(2,1)S(1)} %fusion.38), channel_id=1, source_target_pairs={{0,4},{1,5},{2,6},{3,7},{4,0},{5,1},{6,2},{7,3},{8,12},{9,13},{10,... | collective-permute-start | bytes 884744 | tf_op jit(solution)/shard_map/ppermute | solution.py:42
  179.1 23.8 %collective-permute-start.12 = (bf16[96,1536]{1,0:T(8,128)(2,1)}, bf16[96,1536]{1,0:T(8,128)(2,1)}, u32[]{:S(2)}, u32[]{:S(2)}) collective-permute-start(bf16[96,1536]{1,0:T(8,128)(2,1)} %fusion.35), channel_id=1, source_target_pairs={{0,2},{1,3},{2,0},{3,1},{4,6},{5,7},{6,4},{7,5},{8,10},{9,11},{10,... | collective-permute-start | bytes 884744 | tf_op jit(solution)/shard_map/ppermute | solution.py:42
  179.6 23.3 %collective-permute-start.13 = (bf16[96,1536]{1,0:T(8,128)(2,1)}, bf16[96,1536]{1,0:T(8,128)(2,1)}, u32[]{:S(2)}, u32[]{:S(2)}) collective-permute-start(bf16[96,1536]{1,0:T(8,128)(2,1)} %fusion.36), channel_id=1, source_target_pairs={{0,4},{1,5},{2,6},{3,7},{4,0},{5,1},{6,2},{7,3},{8,12},{9,13},{10,... | collective-permute-start | bytes 884744 | tf_op jit(solution)/shard_map/ppermute | solution.py:42
  196.6 29.6 %collective-permute-start.26 = (bf16[192,1536]{1,0:T(8,128)(2,1)}, bf16[192,1536]{1,0:T(8,128)(2,1)}, u32[]{:S(2)}, u32[]{:S(2)}) collective-permute-start(bf16[192,1536]{1,0:T(8,128)(2,1)} %pad_maximum_fusion.6), channel_id=1, source_target_pairs={{0,4},{1,5},{2,6},{3,7},{4,0},{5,1},{6,2},{7,3},{8,12},{9,13},{10,... | collective-permute-start | bytes 1769480 | tf_op jit(solution)/shard_map/ppermute | solution.py:42
  198.6 31.5 %collective-permute-start.28 = (bf16[192,1536]{1,0:T(8,128)(2,1)}, bf16[192,1536]{1,0:T(8,128)(2,1)}, u32[]{:S(2)}, u32[]{:S(2)}) collective-permute-start(bf16[192,1536]{1,0:T(8,128)(2,1)} %pad_maximum_fusion.7), channel_id=1, source_target_pairs={{0,2},{1,3},{2,0},{3,1},{4,6},{5,7},{6,4},{7,5},{8,10},{9,11},{10,... | collective-permute-start | bytes 1769480 | tf_op jit(solution)/shard_map/ppermute | solution.py:42
  207.7 6.6 %collective-permute-start.18 = (bf16[2,48,768]{2,1,0:T(8,128)(2,1)S(1)}, bf16[2,48,768]{2,1,0:T(8,128)(2,1)S(1)}, u32[]{:S(2)}, u32[]{:S(2)}) collective-permute-start(bf16[2,48,768]{2,1,0:T(8,128)(2,1)S(1)} %fusion.58), channel_id=1, source_target_pairs={{0,16},{1,17},{2,18},{3,19},{4,20},{5,21},{6,22},{7,23},{8,24},{9,... | collective-permute-start | bytes 442376 | tf_op jit(solution)/shard_map/ppermute | solution.py:42
  208.1 8.7 %collective-permute-start.16 = (bf16[2,48,1536]{2,1,0:T(8,128)(2,1)S(1)}, bf16[2,48,1536]{2,1,0:T(8,128)(2,1)S(1)}, u32[]{:S(2)}, u32[]{:S(2)}) collective-permute-start(bf16[2,48,1536]{2,1,0:T(8,128)(2,1)S(1)} %pad_maximum_fusion.17), channel_id=1, source_target_pairs={{0,8},{1,9},{2,10},{3,11},{4,12},{5,13},{6,14},{7,15},{8,0},{9,1},... | collective-permute-start | bytes 884744 | tf_op jit(solution)/shard_map/ppermute | solution.py:42
  214.4 11.5 %collective-permute-start.53 = (bf16[2,48,768]{2,1,0:T(8,128)(2,1)S(1)}, bf16[2,48,768]{2,1,0:T(8,128)(2,1)S(1)}, u32[]{:S(2)}, u32[]{:S(2)}) collective-permute-start(bf16[2,48,768]{2,1,0:T(8,128)(2,1)S(1)} %fusion.50), channel_id=1, source_target_pairs={{0,16},{1,17},{2,18},{3,19},{4,20},{5,21},{6,22},{7,23},{8,24},{9,... | collective-permute-start | bytes 442376 | tf_op jit(solution)/shard_map/ppermute | solution.py:42
  217.5 14.2 %collective-permute-start.42 = (bf16[2,24,1536]{2,1,0:T(8,128)(2,1)S(1)}, bf16[2,24,1536]{2,1,0:T(8,128)(2,1)S(1)}, u32[]{:S(2)}, u32[]{:S(2)}) collective-permute-start(bf16[2,24,1536]{2,1,0:T(8,128)(2,1)S(1)} %fusion.60), channel_id=1, source_target_pairs={{0,16},{1,17},{2,18},{3,19},{4,20},{5,21},{6,22},{7,23},{8,24},{9,... | collective-permute-start | bytes 442376 | tf_op jit(solution)/shard_map/ppermute | solution.py:42
  217.7 14.4 %collective-permute-start.21 = (f32[88,768]{1,0:T(8,128)S(1)}, f32[88,768]{1,0:T(8,128)S(1)}, u32[]{:S(2)}, u32[]{:S(2)}) collective-permute-start(f32[88,768]{1,0:T(8,128)S(1)} %pad_maximum_fusion.23), channel_id=1, source_target_pairs={{0,1},{1,0},{2,3},{3,2},{4,5},{5,4},{6,7},{7,6},{8,9},{9,8},{10,11... | collective-permute-start | bytes 811016 | tf_op jit(solution)/shard_map/ppermute | solution.py:42
  226.0 16.2 %collective-permute-start.54 = (bf16[2,96,768]{2,1,0:T(8,128)(2,1)S(1)}, bf16[2,96,768]{2,1,0:T(8,128)(2,1)S(1)}, u32[]{:S(2)}, u32[]{:S(2)}) collective-permute-start(bf16[2,96,768]{2,1,0:T(8,128)(2,1)S(1)} %pad_maximum_fusion.22), channel_id=1, source_target_pairs={{0,8},{1,9},{2,10},{3,11},{4,12},{5,13},{6,14},{7,15},{8,0},{9,1},... | collective-permute-start | bytes 884744 | tf_op jit(solution)/shard_map/ppermute | solution.py:42
  226.2 38.6 %collective-permute-start.19 = (bf16[8,64,768]{2,1,0:T(8,128)(2,1)S(1)}, bf16[8,64,768]{2,1,0:T(8,128)(2,1)S(1)}, u32[]{:S(2)}, u32[]{:S(2)}) collective-permute-start(bf16[8,64,768]{2,1,0:T(8,128)(2,1)S(1)} %fusion.18), channel_id=1, source_target_pairs={{0,1},{1,0},{2,3},{3,2},{4,5},{5,4},{6,7},{7,6},{8,9},{9,8},{10,11... | collective-permute-start | bytes 2359304 | tf_op jit(solution)/shard_map/ppermute | solution.py:42
  230.1 12.3 %collective-permute-start.27 = (bf16[96,1536]{1,0:T(8,128)(2,1)S(1)}, bf16[96,1536]{1,0:T(8,128)(2,1)S(1)}, u32[]{:S(2)}, u32[]{:S(2)}) collective-permute-start(bf16[96,1536]{1,0:T(8,128)(2,1)S(1)} %fusion.39), channel_id=1, source_target_pairs={{0,2},{1,3},{2,0},{3,1},{4,6},{5,7},{6,4},{7,5},{8,10},{9,11},{10,... | collective-permute-start | bytes 884744 | tf_op jit(solution)/shard_map/ppermute | solution.py:42
  231.7 11.3 %collective-permute-start.29 = (bf16[96,1536]{1,0:T(8,128)(2,1)S(1)}, bf16[96,1536]{1,0:T(8,128)(2,1)S(1)}, u32[]{:S(2)}, u32[]{:S(2)}) collective-permute-start(bf16[96,1536]{1,0:T(8,128)(2,1)S(1)} %fusion.40), channel_id=1, source_target_pairs={{0,4},{1,5},{2,6},{3,7},{4,0},{5,1},{6,2},{7,3},{8,12},{9,13},{10,... | collective-permute-start | bytes 884744 | tf_op jit(solution)/shard_map/ppermute | solution.py:42
  232.1 8.9 %collective-permute-start.43 = (bf16[2,24,1536]{2,1,0:T(8,128)(2,1)S(1)}, bf16[2,24,1536]{2,1,0:T(8,128)(2,1)S(1)}, u32[]{:S(2)}, u32[]{:S(2)}) collective-permute-start(bf16[2,24,1536]{2,1,0:T(8,128)(2,1)S(1)} %fusion.51), channel_id=1, source_target_pairs={{0,16},{1,17},{2,18},{3,19},{4,20},{5,21},{6,22},{7,23},{8,24},{9,... | collective-permute-start | bytes 442376 | tf_op jit(solution)/shard_map/ppermute | solution.py:42
  241.0 6.4 %collective-permute-start.22 = (f32[88,768]{1,0:T(8,128)S(1)}, f32[88,768]{1,0:T(8,128)S(1)}, u32[]{:S(2)}, u32[]{:S(2)}) collective-permute-start(f32[88,768]{1,0:T(8,128)S(1)} %fusion.82), channel_id=1, source_target_pairs={{0,4},{1,5},{2,6},{3,7},{4,0},{5,1},{6,2},{7,3},{8,12},{9,13},{10,... | collective-permute-start | bytes 811016 | tf_op jit(solution)/shard_map/ppermute | solution.py:42
  242.2 8.5 %collective-permute-start.44 = (bf16[2,48,1536]{2,1,0:T(8,128)(2,1)S(1)}, bf16[2,48,1536]{2,1,0:T(8,128)(2,1)S(1)}, u32[]{:S(2)}, u32[]{:S(2)}) collective-permute-start(bf16[2,48,1536]{2,1,0:T(8,128)(2,1)S(1)} %pad_maximum_fusion.21), channel_id=1, source_target_pairs={{0,8},{1,9},{2,10},{3,11},{4,12},{5,13},{6,14},{7,15},{8,0},{9,1},... | collective-permute-start | bytes 884744 | tf_op jit(solution)/shard_map/ppermute | solution.py:42
  242.4 12.1 %collective-permute-start.57 = (bf16[192,768]{1,0:T(8,128)(2,1)S(1)}, bf16[192,768]{1,0:T(8,128)(2,1)S(1)}, u32[]{:S(2)}, u32[]{:S(2)}) collective-permute-start(bf16[192,768]{1,0:T(8,128)(2,1)S(1)} %get-tuple-element.140), channel_id=1, source_target_pairs={{0,4},{1,5},{2,6},{3,7},{4,0},{5,1},{6,2},{7,3},{8,12},{9,13},{10,... | collective-permute-start | bytes 884744 | tf_op jit(solution)/shard_map/ppermute | solution.py:42
  243.0 6.5 %collective-permute-start.55 = (bf16[192,768]{1,0:T(8,128)(2,1)S(1)}, bf16[192,768]{1,0:T(8,128)(2,1)S(1)}, u32[]{:S(2)}, u32[]{:S(2)}) collective-permute-start(bf16[192,768]{1,0:T(8,128)(2,1)S(1)} %get-tuple-element.141), channel_id=1, source_target_pairs={{0,2},{1,3},{2,0},{3,1},{4,6},{5,7},{6,4},{7,5},{8,10},{9,11},{10,... | collective-permute-start | bytes 884744 | tf_op jit(solution)/shard_map/ppermute | solution.py:42
  247.4 8.4 %collective-permute-start.30 = (bf16[2,48,1536]{2,1,0:T(8,128)(2,1)S(1)}, bf16[2,48,1536]{2,1,0:T(8,128)(2,1)S(1)}, u32[]{:S(2)}, u32[]{:S(2)}) collective-permute-start(bf16[2,48,1536]{2,1,0:T(8,128)(2,1)S(1)} %pad_maximum_fusion.19), channel_id=1, source_target_pairs={{0,8},{1,9},{2,10},{3,11},{4,12},{5,13},{6,14},{7,15},{8,0},{9,1},... | collective-permute-start | bytes 884744 | tf_op jit(solution)/shard_map/ppermute | solution.py:42
  249.5 27.1 %collective-permute-start.23 = (f32[88,768]{1,0:T(8,128)}, f32[88,768]{1,0:T(8,128)}, u32[]{:S(2)}, u32[]{:S(2)}) collective-permute-start(f32[88,768]{1,0:T(8,128)} %add.380), channel_id=1, source_target_pairs={{0,2},{1,3},{2,0},{3,1},{4,6},{5,7},{6,4},{7,5},{8,10},{9,11},{10,... | collective-permute-start | bytes 811016 | tf_op jit(solution)/shard_map/ppermute | solution.py:42
  250.7 75.8 %collective-permute-start.61 = (bf16[384,768]{1,0:T(8,128)(2,1)S(1)}, bf16[384,768]{1,0:T(8,128)(2,1)}, u32[]{:S(2)}, u32[]{:S(2)}) collective-permute-start(bf16[384,768]{1,0:T(8,128)(2,1)S(1)} %pad_maximum_fusion.12.refs_1_), channel_id=1, source_target_pairs={{0,1},{1,0},{2,3},{3,2},{4,5},{5,4},{6,7},{7,6},{8,9},{9,8},{10,11... | collective-permute-start | bytes 1769480 | tf_op jit(solution)/shard_map/ppermute | solution.py:42
  254.5 95.4 %collective-permute-start.56 = (bf16[384,768]{1,0:T(8,128)(2,1)S(1)}, bf16[384,768]{1,0:T(8,128)(2,1)S(1)}, u32[]{:S(2)}, u32[]{:S(2)}) collective-permute-start(bf16[384,768]{1,0:T(8,128)(2,1)S(1)} %pad_maximum_fusion.12.refs_1_), channel_id=1, source_target_pairs={{0,4},{1,5},{2,6},{3,7},{4,0},{5,1},{6,2},{7,3},{8,12},{9,13},{10,... | collective-permute-start | bytes 1769480 | tf_op jit(solution)/shard_map/ppermute | solution.py:42
  255.9 8.1 %collective-permute-start.31 = (bf16[2,24,1536]{2,1,0:T(8,128)(2,1)S(1)}, bf16[2,24,1536]{2,1,0:T(8,128)(2,1)S(1)}, u32[]{:S(2)}, u32[]{:S(2)}) collective-permute-start(bf16[2,24,1536]{2,1,0:T(8,128)(2,1)S(1)} %fusion.59), channel_id=1, source_target_pairs={{0,16},{1,17},{2,18},{3,19},{4,20},{5,21},{6,22},{7,23},{8,24},{9,... | collective-permute-start | bytes 442376 | tf_op jit(solution)/shard_map/ppermute | solution.py:42
  264.0 17.1 %collective-permute-start.47 = (bf16[96,1536]{1,0:T(8,128)(2,1)}, bf16[96,1536]{1,0:T(8,128)(2,1)}, u32[]{:S(2)}, u32[]{:S(2)}) collective-permute-start(bf16[96,1536]{1,0:T(8,128)(2,1)} %get-tuple-element.148), channel_id=1, source_target_pairs={{0,4},{1,5},{2,6},{3,7},{4,0},{5,1},{6,2},{7,3},{8,12},{9,13},{10,... | collective-permute-start | bytes 884744 | tf_op jit(solution)/shard_map/ppermute | solution.py:42
  264.7 17.9 %collective-permute-start.45 = (bf16[96,1536]{1,0:T(8,128)(2,1)S(1)}, bf16[96,1536]{1,0:T(8,128)(2,1)}, u32[]{:S(2)}, u32[]{:S(2)}) collective-permute-start(bf16[96,1536]{1,0:T(8,128)(2,1)S(1)} %get-tuple-element.149), channel_id=1, source_target_pairs={{0,2},{1,3},{2,0},{3,1},{4,6},{5,7},{6,4},{7,5},{8,10},{9,11},{10,... | collective-permute-start | bytes 884744 | tf_op jit(solution)/shard_map/ppermute | solution.py:42
  267.7 107.4 %all-to-all-start.2 = ((bf16[8,64,1536]{2,1,0:T(8,128)(2,1)}), bf16[8,64,1536]{2,1,0:T(8,128)(2,1)}, u32[]{:S(2)}, u32[]{:S(2)}) async-start(bf16[8,64,1536]{2,1,0:T(8,128)(2,1)} %pad_maximum_fusion.4), calls=%async_computation.2 | async-start | bytes 3145728 | tf_op jit(solution)/shard_map/all_to_all | solution.py:57
  276.5 51.3 %collective-permute-start.62 = (bf16[384,768]{1,0:T(8,128)(2,1)S(1)}, bf16[384,768]{1,0:T(8,128)(2,1)S(1)}, u32[]{:S(2)}, u32[]{:S(2)}) collective-permute-start(bf16[384,768]{1,0:T(8,128)(2,1)S(1)} %pad_maximum_fusion.13.refs_2_), channel_id=1, source_target_pairs={{0,1},{1,0},{2,3},{3,2},{4,5},{5,4},{6,7},{7,6},{8,9},{9,8},{10,11... | collective-permute-start | bytes 1769480 | tf_op jit(solution)/shard_map/ppermute | solution.py:42
  281.1 37.0 %collective-permute-start.32 = (bf16[2,24,1536]{2,1,0:T(8,128)(2,1)S(1)}, bf16[2,24,1536]{2,1,0:T(8,128)(2,1)S(1)}, u32[]{:S(2)}, u32[]{:S(2)}) collective-permute-start(bf16[2,24,1536]{2,1,0:T(8,128)(2,1)S(1)} %copy-done.59), channel_id=1, source_target_pairs={{0,16},{1,17},{2,18},{3,19},{4,20},{5,21},{6,22},{7,23},{8,24},{9,... | collective-permute-start | bytes 442376 | tf_op jit(solution)/shard_map/ppermute | solution.py:42
  282.6 35.8 %collective-permute-start.24 = (f32[88,768]{1,0:T(8,128)S(1)}, f32[88,768]{1,0:T(8,128)S(1)}, u32[]{:S(2)}, u32[]{:S(2)}) collective-permute-start(f32[88,768]{1,0:T(8,128)S(1)} %add.381), channel_id=1, source_target_pairs={{0,8},{1,9},{2,10},{3,11},{4,12},{5,13},{6,14},{7,15},{8,0},{9,1},... | collective-permute-start | bytes 811016 | tf_op jit(solution)/shard_map/ppermute | solution.py:42
  318.2 8.2 %collective-permute-start.33 = (bf16[2,48,1536]{2,1,0:T(8,128)(2,1)S(1)}, bf16[2,48,1536]{2,1,0:T(8,128)(2,1)S(1)}, u32[]{:S(2)}, u32[]{:S(2)}) collective-permute-start(bf16[2,48,1536]{2,1,0:T(8,128)(2,1)S(1)} %pad_maximum_fusion.20), channel_id=1, source_target_pairs={{0,8},{1,9},{2,10},{3,11},{4,12},{5,13},{6,14},{7,15},{8,0},{9,1},... | collective-permute-start | bytes 884744 | tf_op jit(solution)/shard_map/ppermute | solution.py:42
  318.4 33.2 %collective-permute-start.58 = (bf16[384,768]{1,0:T(8,128)(2,1)S(1)}, bf16[384,768]{1,0:T(8,128)(2,1)S(1)}, u32[]{:S(2)}, u32[]{:S(2)}) collective-permute-start(bf16[384,768]{1,0:T(8,128)(2,1)S(1)} %pad_maximum_fusion.13.refs_2_), channel_id=1, source_target_pairs={{0,2},{1,3},{2,0},{3,1},{4,6},{5,7},{6,4},{7,5},{8,10},{9,11},{10,... | collective-permute-start | bytes 1769480 | tf_op jit(solution)/shard_map/ppermute | solution.py:42
  326.3 15.1 %collective-permute-start.25 = (f32[88,768]{1,0:T(8,128)S(1)}, f32[88,768]{1,0:T(8,128)S(1)}, u32[]{:S(2)}, u32[]{:S(2)}) collective-permute-start(f32[88,768]{1,0:T(8,128)S(1)} %add.382), channel_id=1, source_target_pairs={{0,16},{1,17},{2,18},{3,19},{4,20},{5,21},{6,22},{7,23},{8,24},{9,... | collective-permute-start | bytes 811016 | tf_op jit(solution)/shard_map/ppermute | solution.py:42
  326.5 34.4 %collective-permute-start.51 = (bf16[192,1536]{1,0:T(8,128)(2,1)S(1)}, bf16[192,1536]{1,0:T(8,128)(2,1)S(1)}, u32[]{:S(2)}, u32[]{:S(2)}) collective-permute-start(bf16[192,1536]{1,0:T(8,128)(2,1)S(1)} %pad_maximum_fusion.10.refs_1_), channel_id=1, source_target_pairs={{0,1},{1,0},{2,3},{3,2},{4,5},{5,4},{6,7},{7,6},{8,9},{9,8},{10,11... | collective-permute-start | bytes 1769480 | tf_op jit(solution)/shard_map/ppermute | solution.py:42
  327.9 33.2 %collective-permute-start.46 = (bf16[192,1536]{1,0:T(8,128)(2,1)S(1)}, bf16[192,1536]{1,0:T(8,128)(2,1)}, u32[]{:S(2)}, u32[]{:S(2)}) collective-permute-start(bf16[192,1536]{1,0:T(8,128)(2,1)S(1)} %pad_maximum_fusion.10.refs_1_), channel_id=1, source_target_pairs={{0,4},{1,5},{2,6},{3,7},{4,0},{5,1},{6,2},{7,3},{8,12},{9,13},{10,... | collective-permute-start | bytes 1769480 | tf_op jit(solution)/shard_map/ppermute | solution.py:42
  341.4 8.0 %collective-permute-start.36 = (bf16[96,1536]{1,0:T(8,128)(2,1)S(1)}, bf16[96,1536]{1,0:T(8,128)(2,1)S(1)}, u32[]{:S(2)}, u32[]{:S(2)}) collective-permute-start(bf16[96,1536]{1,0:T(8,128)(2,1)S(1)} %get-tuple-element.156), channel_id=1, source_target_pairs={{0,4},{1,5},{2,6},{3,7},{4,0},{5,1},{6,2},{7,3},{8,12},{9,13},{10,... | collective-permute-start | bytes 884744 | tf_op jit(solution)/shard_map/ppermute | solution.py:42
  349.4 7.1 %collective-permute-start.34 = (bf16[96,1536]{1,0:T(8,128)(2,1)S(1)}, bf16[96,1536]{1,0:T(8,128)(2,1)S(1)}, u32[]{:S(2)}, u32[]{:S(2)}) collective-permute-start(bf16[96,1536]{1,0:T(8,128)(2,1)S(1)} %get-tuple-element.157), channel_id=1, source_target_pairs={{0,2},{1,3},{2,0},{3,1},{4,6},{5,7},{6,4},{7,5},{8,10},{9,11},{10,... | collective-permute-start | bytes 884744 | tf_op jit(solution)/shard_map/ppermute | solution.py:42
  349.9 11.3 %collective-permute-start.52 = (bf16[192,1536]{1,0:T(8,128)(2,1)S(1)}, bf16[192,1536]{1,0:T(8,128)(2,1)S(1)}, u32[]{:S(2)}, u32[]{:S(2)}) collective-permute-start(bf16[192,1536]{1,0:T(8,128)(2,1)S(1)} %pad_maximum_fusion.11.refs_2_), channel_id=1, source_target_pairs={{0,1},{1,0},{2,3},{3,2},{4,5},{5,4},{6,7},{7,6},{8,9},{9,8},{10,11... | collective-permute-start | bytes 1769480 | tf_op jit(solution)/shard_map/ppermute | solution.py:42
  351.6 17.7 %collective-permute-start.48 = (bf16[192,1536]{1,0:T(8,128)(2,1)S(1)}, bf16[192,1536]{1,0:T(8,128)(2,1)}, u32[]{:S(2)}, u32[]{:S(2)}) collective-permute-start(bf16[192,1536]{1,0:T(8,128)(2,1)S(1)} %pad_maximum_fusion.11.refs_2_), channel_id=1, source_target_pairs={{0,2},{1,3},{2,0},{3,1},{4,6},{5,7},{6,4},{7,5},{8,10},{9,11},{10,... | collective-permute-start | bytes 1769480 | tf_op jit(solution)/shard_map/ppermute | solution.py:42
  356.5 17.0 %collective-permute-start.59 = (bf16[384,768]{1,0:T(8,128)(2,1)S(1)}, bf16[384,768]{1,0:T(8,128)(2,1)S(1)}, u32[]{:S(2)}, u32[]{:S(2)}) collective-permute-start(bf16[384,768]{1,0:T(8,128)(2,1)S(1)} %collective-permute-done.56.refs_1_), channel_id=1, source_target_pairs={{0,1},{1,0},{2,3},{3,2},{4,5},{5,4},{6,7},{7,6},{8,9},{9,8},{10,11... | collective-permute-start | bytes 1769480 | tf_op jit(solution)/shard_map/ppermute | solution.py:42
  360.9 15.5 %collective-permute-start.60 = (bf16[384,768]{1,0:T(8,128)(2,1)S(1)}, bf16[384,768]{1,0:T(8,128)(2,1)}, u32[]{:S(2)}, u32[]{:S(2)}) collective-permute-start(bf16[384,768]{1,0:T(8,128)(2,1)S(1)} %collective-permute-done.58.refs_2_), channel_id=1, source_target_pairs={{0,1},{1,0},{2,3},{3,2},{4,5},{5,4},{6,7},{7,6},{8,9},{9,8},{10,11... | collective-permute-start | bytes 1769480 | tf_op jit(solution)/shard_map/ppermute | solution.py:42
  361.0 17.3 %collective-permute-start.35 = (bf16[192,1536]{1,0:T(8,128)(2,1)S(1)}, bf16[192,1536]{1,0:T(8,128)(2,1)}, u32[]{:S(2)}, u32[]{:S(2)}) collective-permute-start(bf16[192,1536]{1,0:T(8,128)(2,1)S(1)} %pad_maximum_fusion.8.refs_1_), channel_id=1, source_target_pairs={{0,4},{1,5},{2,6},{3,7},{4,0},{5,1},{6,2},{7,3},{8,12},{9,13},{10,... | collective-permute-start | bytes 1769480 | tf_op jit(solution)/shard_map/ppermute | solution.py:42
  362.0 19.9 %collective-permute-start.37 = (bf16[192,1536]{1,0:T(8,128)(2,1)S(1)}, bf16[192,1536]{1,0:T(8,128)(2,1)}, u32[]{:S(2)}, u32[]{:S(2)}) collective-permute-start(bf16[192,1536]{1,0:T(8,128)(2,1)S(1)} %pad_maximum_fusion.9.refs_2_), channel_id=1, source_target_pairs={{0,2},{1,3},{2,0},{3,1},{4,6},{5,7},{6,4},{7,5},{8,10},{9,11},{10,... | collective-permute-start | bytes 1769480 | tf_op jit(solution)/shard_map/ppermute | solution.py:42
  369.3 15.0 %collective-permute-start.49 = (bf16[192,1536]{1,0:T(8,128)(2,1)}, bf16[192,1536]{1,0:T(8,128)(2,1)}, u32[]{:S(2)}, u32[]{:S(2)}) collective-permute-start(bf16[192,1536]{1,0:T(8,128)(2,1)} %collective-permute-done.46.refs_1_), channel_id=1, source_target_pairs={{0,1},{1,0},{2,3},{3,2},{4,5},{5,4},{6,7},{7,6},{8,9},{9,8},{10,11... | collective-permute-start | bytes 1769480 | tf_op jit(solution)/shard_map/ppermute | solution.py:42
  374.4 9.8 %collective-permute-start.50 = (bf16[192,1536]{1,0:T(8,128)(2,1)}, bf16[192,1536]{1,0:T(8,128)(2,1)}, u32[]{:S(2)}, u32[]{:S(2)}) collective-permute-start(bf16[192,1536]{1,0:T(8,128)(2,1)} %collective-permute-done.48.refs_2_), channel_id=1, source_target_pairs={{0,1},{1,0},{2,3},{3,2},{4,5},{5,4},{6,7},{7,6},{8,9},{9,8},{10,11... | collective-permute-start | bytes 1769480 | tf_op jit(solution)/shard_map/ppermute | solution.py:42
  376.4 32.4 %collective-permute-start.20 = (bf16[4,64,1536]{2,1,0:T(8,128)(2,1)S(1)}, bf16[4,64,1536]{2,1,0:T(8,128)(2,1)S(1)}, u32[]{:S(2)}, u32[]{:S(2)}) collective-permute-start(bf16[4,64,1536]{2,1,0:T(8,128)(2,1)S(1)} %dynamic-slice_bitcast_fusion.2), channel_id=1, source_target_pairs={{0,1},{1,0},{2,3},{3,2},{4,5},{5,4},{6,7},{7,6},{8,9},{9,8},{10,11... | collective-permute-start | bytes 2359304 | tf_op jit(solution)/shard_map/ppermute | solution.py:42
  378.3 23.8 %collective-permute-start.40 = (bf16[192,1536]{1,0:T(8,128)(2,1)S(1)}, bf16[192,1536]{1,0:T(8,128)(2,1)S(1)}, u32[]{:S(2)}, u32[]{:S(2)}) collective-permute-start(bf16[192,1536]{1,0:T(8,128)(2,1)S(1)} %pad_maximum_fusion.8.refs_1_), channel_id=1, source_target_pairs={{0,1},{1,0},{2,3},{3,2},{4,5},{5,4},{6,7},{7,6},{8,9},{9,8},{10,11... | collective-permute-start | bytes 1769480 | tf_op jit(solution)/shard_map/ppermute | solution.py:42
  381.9 20.2 %collective-permute-start.41 = (bf16[192,1536]{1,0:T(8,128)(2,1)S(1)}, bf16[192,1536]{1,0:T(8,128)(2,1)S(1)}, u32[]{:S(2)}, u32[]{:S(2)}) collective-permute-start(bf16[192,1536]{1,0:T(8,128)(2,1)S(1)} %pad_maximum_fusion.9.refs_2_), channel_id=1, source_target_pairs={{0,1},{1,0},{2,3},{3,2},{4,5},{5,4},{6,7},{7,6},{8,9},{9,8},{10,11... | collective-permute-start | bytes 1769480 | tf_op jit(solution)/shard_map/ppermute | solution.py:42
  384.2 20.9 %collective-permute-start.38 = (bf16[192,1536]{1,0:T(8,128)(2,1)}, bf16[192,1536]{1,0:T(8,128)(2,1)S(1)}, u32[]{:S(2)}, u32[]{:S(2)}) collective-permute-start(bf16[192,1536]{1,0:T(8,128)(2,1)} %collective-permute-done.35.refs_1_), channel_id=1, source_target_pairs={{0,1},{1,0},{2,3},{3,2},{4,5},{5,4},{6,7},{7,6},{8,9},{9,8},{10,11... | collective-permute-start | bytes 1769480 | tf_op jit(solution)/shard_map/ppermute | solution.py:42
  384.2 20.9 %collective-permute-start.39 = (bf16[192,1536]{1,0:T(8,128)(2,1)}, bf16[192,1536]{1,0:T(8,128)(2,1)S(1)}, u32[]{:S(2)}, u32[]{:S(2)}) collective-permute-start(bf16[192,1536]{1,0:T(8,128)(2,1)} %collective-permute-done.37.refs_2_), channel_id=1, source_target_pairs={{0,1},{1,0},{2,3},{3,2},{4,5},{5,4},{6,7},{7,6},{8,9},{9,8},{10,11... | collective-permute-start | bytes 1769480 | tf_op jit(solution)/shard_map/ppermute | solution.py:42
  (83 other events, 488.7 us)
